TPU v7x, 256 devices: a whole 4x4x8 slice. The times are simulated.
256 devices in a mesh: tile: 32 (over y, x, core), rep: 8 (over z).
Axes of the slice: x: 4, y: 4, z: 8, core: 2. Of those that a mesh axis runs over, the one named last changes fastest.
Arguments:
- input_video: bfloat16 [8, 24, 256, 64, 128], P('rep', None, 'tile'), may hold values from -60 to 60
- block_clip: int32 [8, 6], P('rep'), may hold values from 0 to 2, as said below
- send_slot: int32 [8, 32, 32, 2], P('rep', 'tile'), may hold values from 0 to 48, as said below
- recv_index: int32 [8, 32, 16], P('rep', 'tile'), may hold values from 0 to 63, as said below
- tile_clip: int32 [8, 32, 16], P('rep', 'tile'), may hold values from 0 to 2, as said below
- kernel: bfloat16 [3456, 256], replicated, may hold values from -0.109375 to 0.109375
- norm_gain: float32 [256], replicated, may hold values from 0.5 to 1.5
- norm_shift: float32 [256], replicated, may hold values from -3 to 3
- upstream: bfloat16 [8, 32, 16, 256, 256], P('rep', 'tile'), may hold values from -26 to 26
Outputs:
- activation: bfloat16 [8, 32, 16, 256, 256], P('rep', 'tile')
- kernel_grad: float32 [3456, 256], P('tile')
- norm_grads: float32 [2, 256], replicated
Inputs may be any that keep to these rules, and one draw needn't show every extreme that they name: block_clip never falls, starts at 0 and each of the 3 clips holds one or more whole time blocks. send_slot[r, t, w, p] is a slot of owner t that goes to worker w in position p, or 48 for none; an owner names each slot at most once; each worker gets exactly 16 tiles from all owners together; in each replica the last owner sends all 48 slots. recv_index[r, w, j] = t * 2 + p for a non-empty send_slot[r, t, w, p]; a worker's entries are distinct and cover all such entries addressed to it. tile_clip[r, w, j] is block_clip of the time block of work tile j.
All inputs are finite; a program needn't handle non-finite values.
Results may differ from a plain program's by a relative error of at most 0.0029.
Values may be sent and summed in bfloat16 or wider, within the bound.
A program may use at most 128 MiB of HBM per device.

v0:
```python
from functools import partial

import jax
import jax.numpy as jnp
from jax import lax
from jax.sharding import PartitionSpec as P

C_IN = 128
C_OUT = 256
GROUPS = 32
CPG = 8
TT = 4
TH = 8
TW = 8
TBLK = 6
CLIPS = 3
WBLK = 8
WSLOTS = 16
VOX = 256


epsilon = 1e-05
highest = lax.Precision.HIGHEST


def extended(cells, sides, width):
    for axis, dim in sides:
        count = lax.axis_size(axis)
        ends = count - 1
        head = lax.slice_in_dim(cells, 0, width, axis=dim)
        tail = lax.slice_in_dim(cells, cells.shape[dim] - width, cells.shape[dim], axis=dim)
        cells = jnp.concatenate(
            [
                lax.ppermute(tail, axis, [(i, (i + 1) % count) for i in range(ends)]),
                cells,
                lax.ppermute(head, axis, [((i + 1) % count, i) for i in range(ends)]),
            ],
            axis=dim,
        )
    return cells


def cut_tile(padded, clip_ids, strip_row, slot_id):
    block_id = slot_id // WBLK
    width_block = slot_id % WBLK
    zero_start = jnp.zeros((), jnp.int32)
    section = lax.dynamic_slice(
        padded,
        (block_id * TT, strip_row, width_block * TW, zero_start),
        (TT + 2, TH + 2, TW + 2, C_IN),
    )
    earlier = clip_ids[jnp.maximum(block_id - 1, 0)]
    linked = jnp.logical_and(block_id > 0, earlier == clip_ids[block_id])
    history = jnp.where(linked, section[:2], jnp.zeros_like(section[:2]))
    return jnp.concatenate([history, section[2:]], axis=0)


def unfold(tile_stack):
    columns = []
    for offset_t in range(3):
        for offset_h in range(3):
            for offset_w in range(3):
                columns.append(
                    tile_stack[
                        :,
                        offset_t : offset_t + TT,
                        offset_h : offset_h + TH,
                        offset_w : offset_w + TW,
                        :,
                    ]
                )
    return jnp.stack(columns, axis=4).reshape(-1, 27 * tile_stack.shape[-1])


def group_table(onehot, per_tile):
    return jnp.einsum("sk,sg->kg", onehot, per_tile, precision=highest)


def spread_table(onehot, group_values):
    return jnp.einsum("sk,kg->sg", onehot, group_values, precision=highest)


def shards(
    input_video,
    block_clip,
    send_slot,
    recv_index,
    tile_clip,
    kernel,
    norm_gain,
    norm_shift,
    upstream,
):
    peer_count = lax.axis_size("tile")
    loss_scale = float(lax.axis_size("rep") * peer_count * WSLOTS * VOX) ** (-0.5)
    frames = input_video[0]
    clip_ids = block_clip[0]
    rimmed = extended(frames, (("tile", 1),), 1)
    padded = jnp.pad(rimmed, ((2, 0), (0, 0), (1, 1), (0, 0)))
    send_plan = send_slot[0, 0]
    capacity = send_plan.shape[1]
    chosen = jnp.minimum(send_plan.reshape(-1), TBLK * WBLK - 1)
    zero_rows = jnp.zeros_like(chosen)
    outgoing = jax.vmap(partial(cut_tile, padded, clip_ids))(zero_rows, chosen)
    outgoing = outgoing.reshape((peer_count, capacity) + outgoing.shape[1:])
    arrived = lax.all_to_all(outgoing, "tile", split_axis=0, concat_axis=0, tiled=True)
    arrived = arrived.reshape((peer_count * capacity,) + arrived.shape[2:])
    work_tiles = arrived[recv_index[0, 0]]

    def tile_forward(one_tile):
        return jnp.dot(unfold(one_tile[None]), kernel, preferred_element_type=jnp.float32)

    conv_out = lax.map(tile_forward, work_tiles)
    grouped = conv_out.reshape(-1, VOX, GROUPS, CPG)
    onehot = (tile_clip[0, 0][:, None] == jnp.arange(CLIPS, dtype=jnp.int32)[None, :]).astype(
        jnp.float32
    )
    local_count = jnp.sum(onehot, axis=0) * float(VOX * CPG)
    local_first = group_table(onehot, jnp.sum(grouped, axis=(1, 3)))
    total_first, total_count = lax.psum((local_first, local_count), "tile")
    group_mean = total_first / total_count[:, None]
    centred = grouped - spread_table(onehot, group_mean)[:, None, :, None]
    local_second = group_table(onehot, jnp.sum(centred * centred, axis=(1, 3)))
    variance = lax.psum(local_second, "tile") / total_count[:, None]
    inverse_std = lax.rsqrt(variance + epsilon)
    tile_inverse = spread_table(onehot, inverse_std)[:, None, :, None]
    normed = (centred * tile_inverse).reshape(-1, VOX, C_OUT)
    pre_act = normed * norm_gain + norm_shift
    activation = jax.nn.silu(pre_act).astype(jnp.bfloat16)
    incoming = upstream[0, 0].astype(jnp.float32) * loss_scale
    sigmoid_act = jax.nn.sigmoid(pre_act)
    pre_grad = incoming * sigmoid_act * (1.0 + pre_act * (1.0 - sigmoid_act))
    norm_local = jnp.stack(
        [jnp.sum(pre_grad * normed, axis=(0, 1)), jnp.sum(pre_grad, axis=(0, 1))]
    )
    normed_grad = (pre_grad * norm_gain).reshape(-1, VOX, GROUPS, CPG)
    normed_groups = normed.reshape(-1, VOX, GROUPS, CPG)
    local_grad = group_table(onehot, jnp.sum(normed_grad, axis=(1, 3)))
    local_cross = group_table(onehot, jnp.sum(normed_grad * normed_groups, axis=(1, 3)))
    total_grad, total_cross = lax.psum((local_grad, local_cross), "tile")
    mean_grad = total_grad / total_count[:, None]
    mean_cross = total_cross / total_count[:, None]
    conv_grad = tile_inverse * (
        normed_grad
        - spread_table(onehot, mean_grad)[:, None, :, None]
        - normed_groups * spread_table(onehot, mean_cross)[:, None, :, None]
    )
    conv_grad = conv_grad.reshape(-1, VOX, C_OUT).astype(jnp.bfloat16)
    filter_rows = 27 * C_IN
    row_share = filter_rows // peer_count

    def add_whole(total, item):
        one_tile, tile_grad = item
        return (
            total
            + lax.dot_general(
                unfold(one_tile[None]),
                tile_grad,
                (((0,), (0,)), ((), ())),
                preferred_element_type=jnp.float32,
            ),
            None,
        )

    kernel_local, unused = lax.scan(
        add_whole, jnp.zeros((filter_rows, C_OUT), jnp.float32), (work_tiles, conv_grad)
    )
    kernel_summed, norm_summed = lax.psum((kernel_local, norm_local), ("tile", "rep"))
    strip_index = lax.axis_index("tile")
    grad_shard = lax.dynamic_slice_in_dim(kernel_summed, strip_index * row_share, row_share, 0)
    return (activation.reshape(1, 1, WSLOTS, VOX, C_OUT), grad_shard, norm_summed)


def solution(mesh):
    placed = (
        P("rep", None, "tile", None, None),
        P("rep", None),
        P("rep", "tile", None, None),
        P("rep", "tile", None),
        P("rep", "tile", None),
        P(),
        P(),
        P(),
        P("rep", "tile", None, None, None),
    )
    return jax.shard_map(
        shards,
        mesh=mesh,
        in_specs=placed,
        out_specs=(P("rep", "tile", None, None, None), P("tile", None), P()),
        check_vma=False,
    )
```

profile of v0, /device:TPU:24, one launch (start us, length us, event | category | flops | bytes accessed | tf_op | source)
XLA Modules:
  0.0 2169.8 jit_solution(7954652116806311879)
XLA Ops:
  7.2 4.7 copy.236
  13.7 1.9 collective-permute-start
  16.4 5.7 collective-permute-start.1
  25.2 3.7 bitcast_and_fusion
  29.0 1.8 copy.213
  30.8 1.8 copy.214
  32.5 10.2 fusion.65
  42.8 10.4 gather_fusion
  53.2 3.1 slice_select_fusion
  56.2 2.5 slice-done
  58.7 7.2 pad_maximum_fusion
  65.9 18.0 copy.215
  83.9 5.4 all-to-all-start
  90.2 117.7 %all-to-all-done = bf16[32,2,6,10,10,128]{5,1,4,3,2,0:T(2,128)(2,1)} async-done(((bf16[32,2,6,10,10,128]{5,1,4,3,2,0:T(2,128)(2,1)}), bf16[32,2,6,10,10,128]{5,1,4,3,2,0:T(2,128)(2,1)}, u32[]{:S(2)}, u32[]{:S(2)}) %all-to-all-start) | async-done | bytes 9830432 | tf_op jit(solution)/shard_map/all_to_all | solution.py:106
  207.9 11.3 copy.216
  219.2 7.5 gather_fusion.1
  226.7 4.7 copy.217
  231.4 708.3 %while.21 = (s32[]{:T(128)}, f32[16,256,256]{2,1,0:T(8,128)}, bf16[16,6,10,10,128]{4,3,2,1,0:T(8,128)(2,1)}, bf16[3456,256]{1,0:T(8,128)(2,1)}, s32[]{:T(128)}, /*index=5*/s32[]{:T(128)}, s32[]{}, s32[]{}) while((s32[]{:T(128)}, f32[16,256,256]{2,1,0:T(8,128)}, bf16[16,6,10,10,128]{4,3,2,1,0:T(8,128)(2,1)}, bf16[3456,256]{1,0:T(8,128)(2,1)}, ...), condition=%wide.region_1.2_spmd, body=%wide.region_0.1_spmd.sunk | while | flops 452984832 | bytes 14432037 | solution.py:113
  234.4 1.7 fusion.179
  272.8 2.8 fusion.204
  278.7 1.7 fusion.179
  317.1 2.8 fusion.204
  361.3 2.8 fusion.204
  367.2 1.7 fusion.179
  405.6 2.8 fusion.204
  449.9 2.8 fusion.204
  494.2 2.8 fusion.204
  538.4 2.8 fusion.204
  582.7 2.8 fusion.204
  626.9 2.8 fusion.204
  671.2 2.8 fusion.204
  715.5 2.8 fusion.204
  759.8 2.8 fusion.204
  804.0 2.8 fusion.204
  848.3 2.8 fusion.204
  892.6 2.8 fusion.204
  936.8 2.8 fusion.204
  939.7 2.5 reduce_sum.73
  944.6 53.6 %all-reduce.2 = (f32[3,32]{1,0:T(4,128)S(1)}, f32[3]{0:T(128)S(1)}) all-reduce(f32[3,32]{1,0:T(4,128)S(1)} %fusion.83, f32[3]{0:T(128)} %broadcast_multiply_fusion), channel_id=1, replica_groups=mesh['tile'=32,'rep'=8] {'tile'}, use_global_device_ids=true, to_apply=%region_4.5 | all-reduce | flops 99 | bytes 792 | tf_op jit(solution)/shard_map/psum | solution.py:120
  1000.8 3.2 multiply_reduce_fusion.2
  1007.8 60.6 %psum.51 = f32[3,32]{1,0:T(4,128)} all-reduce(f32[3,32]{1,0:T(4,128)} %fusion.82), channel_id=1, replica_groups=mesh['tile'=32,'rep'=8] {'tile'}, use_global_device_ids=true, to_apply=%region_9.10 | all-reduce | flops 96 | bytes 768 | tf_op jit(solution)/shard_map/psum | solution.py:124
  1071.6 7.7 multiply_reduce_fusion
  1087.0 63.4 %all-reduce.1 = (f32[3,32]{1,0:T(4,128)}, f32[3,32]{1,0:T(4,128)}) all-reduce(f32[3,32]{1,0:T(4,128)} %fusion.80, f32[3,32]{1,0:T(4,128)} %fusion.81), channel_id=1, replica_groups=mesh['tile'=32,'rep'=8] {'tile'}, use_global_device_ids=true, to_apply=%region_15.16 | all-reduce | flops 192 | bytes 1536 | tf_op jit(solution)/shard_map/psum | solution.py:140
  1156.8 6.2 multiply_convert_fusion
  1162.9 713.9 %while.22 = (s32[]{:T(128)}, f32[3456,256]{1,0:T(8,128)S(1)}, bf16[16,6,10,10,128]{4,3,2,1,0:T(8,128)(2,1)}, bf16[16,256,256]{2,1,0:T(8,128)(2,1)}, s32[]{:T(128)}, /*index=5*/s32[]{:T(128)}, s32[]{}, s32[]{}) while((s32[]{:T(128)}, f32[3456,256]{1,0:T(8,128)S(1)}, bf16[16,6,10,10,128]{4,3,2,1,0:T(8,128)(2,1)}, ...), condition=%wide.region_17.18_spmd.clone, body=%wide.region_16.17_spmd.clone.sunk | while | flops 454754304 | bytes 12531475 | solution.py:165
  1204.5 3.0 convolution_add_fusion.2
  1249.1 3.0 convolution_add_fusion.2
  1293.7 3.0 convolution_add_fusion.2
  1338.4 3.0 convolution_add_fusion.2
  1383.0 3.0 convolution_add_fusion.2
  1427.6 3.0 convolution_add_fusion.2
  1472.2 3.0 convolution_add_fusion.2
  1516.9 3.0 convolution_add_fusion.2
  1561.5 3.0 convolution_add_fusion.2
  1606.1 3.0 convolution_add_fusion.2
  1650.7 3.0 convolution_add_fusion.2
  1695.4 3.0 convolution_add_fusion.2
  1740.0 3.0 convolution_add_fusion.2
  1784.6 3.0 convolution_add_fusion.2
  1829.2 3.0 convolution_add_fusion.2
  1873.8 3.0 convolution_add_fusion.2
  1876.9 1.7 copy-done
  1878.7 94.3 %psum.55 = f32[2,256]{1,0:T(2,128)} all-reduce(f32[2,256]{1,0:T(2,128)S(1)} %pad_maximum_fusion.1), channel_id=1, replica_groups=mesh['tile'=32,'rep'=8] {'tile','rep'}, use_global_device_ids=true, to_apply=%region_21.22 | all-reduce | flops 512 | bytes 4096 | tf_op jit(solution)/shard_map/psum | solution.py:168
  1973.0 188.4 %all-reduce.5.cloned.1.call-done = f32[3456,256]{1,0:T(8,128)} async-done(((f32[3456,256]{1,0:T(8,128)}), f32[3456,256]{1,0:T(8,128)}) %all-reduce.5.cloned.1.call-update) | async-done | bytes 3538960 | tf_op jit(solution)/shard_map/psum | solution.py:168
  (954 shorter events, 1356.9 us)
Async XLA Ops:
  11.9 10.3 copy-start.6
  11.9 12.6 copy-start.2
  13.7 15.3 collective-permute-start
  16.4 14.3 collective-permute-start.1
  53.2 5.5 slice-start
  83.9 5.7 copy-start.3
  83.9 5.8 copy-start.7
  83.9 124.0 %all-to-all-start = ((bf16[32,2,6,10,10,128]{5,1,4,3,2,0:T(2,128)(2,1)}), bf16[32,2,6,10,10,128]{5,1,4,3,2,0:T(2,128)(2,1)}, u32[]{:S(2)}, u32[]{:S(2)}) async-start(bf16[32,2,6,10,10,128]{5,1,4,3,2,0:T(2,128)(2,1)} %copy.215), calls=%async_computation | async-start | bytes 19660800 | tf_op jit(solution)/shard_map/all_to_all | solution.py:106
  89.3 2072.1 %all-reduce.5.cloned.1.call-start = ((), (), s32[]{:S(2)}) async-start(), calls=%async_computation.1 | async-start | bytes 7077888 | tf_op jit(solution)/shard_map/psum | solution.py:168
  234.4 38.4 %copy-start.1 = (bf16[3456,256]{1,0:T(8,128)(2,1)S(1)}, bf16[3456,256]{1,0:T(8,128)(2,1)}, u32[]{:S(2)}) copy-start(bf16[3456,256]{1,0:T(8,128)(2,1)} %get-tuple-element.193) | copy-start | bytes 5308420 | tf_op jit(solution)/shard_map/while
  278.7 38.4 %copy-start.1 = (bf16[3456,256]{1,0:T(8,128)(2,1)S(1)}, bf16[3456,256]{1,0:T(8,128)(2,1)}, u32[]{:S(2)}) copy-start(bf16[3456,256]{1,0:T(8,128)(2,1)} %get-tuple-element.193) | copy-start | bytes 5308420 | tf_op jit(solution)/shard_map/while
  322.9 38.4 %copy-start.1 = (bf16[3456,256]{1,0:T(8,128)(2,1)S(1)}, bf16[3456,256]{1,0:T(8,128)(2,1)}, u32[]{:S(2)}) copy-start(bf16[3456,256]{1,0:T(8,128)(2,1)} %get-tuple-element.193) | copy-start | bytes 5308420 | tf_op jit(solution)/shard_map/while
  367.2 38.4 %copy-start.1 = (bf16[3456,256]{1,0:T(8,128)(2,1)S(1)}, bf16[3456,256]{1,0:T(8,128)(2,1)}, u32[]{:S(2)}) copy-start(bf16[3456,256]{1,0:T(8,128)(2,1)} %get-tuple-element.193) | copy-start | bytes 5308420 | tf_op jit(solution)/shard_map/while
  411.5 38.4 %copy-start.1 = (bf16[3456,256]{1,0:T(8,128)(2,1)S(1)}, bf16[3456,256]{1,0:T(8,128)(2,1)}, u32[]{:S(2)}) copy-start(bf16[3456,256]{1,0:T(8,128)(2,1)} %get-tuple-element.193) | copy-start | bytes 5308420 | tf_op jit(solution)/shard_map/while
  455.7 38.4 %copy-start.1 = (bf16[3456,256]{1,0:T(8,128)(2,1)S(1)}, bf16[3456,256]{1,0:T(8,128)(2,1)}, u32[]{:S(2)}) copy-start(bf16[3456,256]{1,0:T(8,128)(2,1)} %get-tuple-element.193) | copy-start | bytes 5308420 | tf_op jit(solution)/shard_map/while
  500.0 38.4 %copy-start.1 = (bf16[3456,256]{1,0:T(8,128)(2,1)S(1)}, bf16[3456,256]{1,0:T(8,128)(2,1)}, u32[]{:S(2)}) copy-start(bf16[3456,256]{1,0:T(8,128)(2,1)} %get-tuple-element.193) | copy-start | bytes 5308420 | tf_op jit(solution)/shard_map/while
  544.3 38.4 %copy-start.1 = (bf16[3456,256]{1,0:T(8,128)(2,1)S(1)}, bf16[3456,256]{1,0:T(8,128)(2,1)}, u32[]{:S(2)}) copy-start(bf16[3456,256]{1,0:T(8,128)(2,1)} %get-tuple-element.193) | copy-start | bytes 5308420 | tf_op jit(solution)/shard_map/while
  588.5 38.4 %copy-start.1 = (bf16[3456,256]{1,0:T(8,128)(2,1)S(1)}, bf16[3456,256]{1,0:T(8,128)(2,1)}, u32[]{:S(2)}) copy-start(bf16[3456,256]{1,0:T(8,128)(2,1)} %get-tuple-element.193) | copy-start | bytes 5308420 | tf_op jit(solution)/shard_map/while
  632.8 38.4 %copy-start.1 = (bf16[3456,256]{1,0:T(8,128)(2,1)S(1)}, bf16[3456,256]{1,0:T(8,128)(2,1)}, u32[]{:S(2)}) copy-start(bf16[3456,256]{1,0:T(8,128)(2,1)} %get-tuple-element.193) | copy-start | bytes 5308420 | tf_op jit(solution)/shard_map/while
  677.1 38.4 %copy-start.1 = (bf16[3456,256]{1,0:T(8,128)(2,1)S(1)}, bf16[3456,256]{1,0:T(8,128)(2,1)}, u32[]{:S(2)}) copy-start(bf16[3456,256]{1,0:T(8,128)(2,1)} %get-tuple-element.193) | copy-start | bytes 5308420 | tf_op jit(solution)/shard_map/while
  721.4 38.4 %copy-start.1 = (bf16[3456,256]{1,0:T(8,128)(2,1)S(1)}, bf16[3456,256]{1,0:T(8,128)(2,1)}, u32[]{:S(2)}) copy-start(bf16[3456,256]{1,0:T(8,128)(2,1)} %get-tuple-element.193) | copy-start | bytes 5308420 | tf_op jit(solution)/shard_map/while
  765.6 38.4 %copy-start.1 = (bf16[3456,256]{1,0:T(8,128)(2,1)S(1)}, bf16[3456,256]{1,0:T(8,128)(2,1)}, u32[]{:S(2)}) copy-start(bf16[3456,256]{1,0:T(8,128)(2,1)} %get-tuple-element.193) | copy-start | bytes 5308420 | tf_op jit(solution)/shard_map/while
  809.9 38.4 %copy-start.1 = (bf16[3456,256]{1,0:T(8,128)(2,1)S(1)}, bf16[3456,256]{1,0:T(8,128)(2,1)}, u32[]{:S(2)}) copy-start(bf16[3456,256]{1,0:T(8,128)(2,1)} %get-tuple-element.193) | copy-start | bytes 5308420 | tf_op jit(solution)/shard_map/while
  854.2 38.4 %copy-start.1 = (bf16[3456,256]{1,0:T(8,128)(2,1)S(1)}, bf16[3456,256]{1,0:T(8,128)(2,1)}, u32[]{:S(2)}) copy-start(bf16[3456,256]{1,0:T(8,128)(2,1)} %get-tuple-element.193) | copy-start | bytes 5308420 | tf_op jit(solution)/shard_map/while
  898.4 38.4 %copy-start.1 = (bf16[3456,256]{1,0:T(8,128)(2,1)S(1)}, bf16[3456,256]{1,0:T(8,128)(2,1)}, u32[]{:S(2)}) copy-start(bf16[3456,256]{1,0:T(8,128)(2,1)} %get-tuple-element.193) | copy-start | bytes 5308420 | tf_op jit(solution)/shard_map/while
  998.2 0.9 copy-start.8
  1876.9 1.8 copy-start
  1876.9 1.8 copy-start.4
  1876.9 1.8 copy-start.5
Sparse Core Ops, SparseCore 0:
  1878.8 282.5 all-reduce.4
where the time goes:
time: 2200 us; the launch traced here: 2170 us
  local copies, waits for them, and re-layouts  1410 us (64%)
  waiting for transfers between devices  306 us (14%)
  blocking collectives  272 us (12%)
  matrix products  102 us (5%)
  other arithmetic  48.3 us (2%)
    while x864, local copies, waits for them, and re-layouts  1280 us
    psum x1, waiting for transfers between devices, shards(): lax.psum((kernel_local, norm_local), ('tile', 'rep'))  188 us
    all_to_all x1, waiting for transfers between devices, shards(): lax.all_to_all(outgoing, 'tile', split_axis=0, concat_axis=0, tiled=True)  118 us
    psum x1, blocking collectives, shards(): lax.psum((kernel_local, norm_local), ('tile', 'rep'))  94.3 us
    psum x1, blocking collectives, shards(): total_grad, total_cross = lax.psum((local_grad, local_cross), 'tile')  63.4 us
    psum x1, blocking collectives, shards(): variance = lax.psum(local_second, 'tile') / total_count[:, None]  60.6 us
    psum x1, blocking collectives, shards(): total_first, total_count = lax.psum((local_first, local_count), 'tile')  53.6 us
    another operation x32, local copies, waits for them, and re-layouts, unfold(): return jnp.stack(columns, axis=4).reshape(-1, 27 * tile_stack.shape[-1])  50.1 us
  transfers between devices with their start and end apart: 4, of which 2 were waited for; matrix products, arithmetic and copies ran while one was open for 0% of the time, Pallas kernels for 0%

commit v1 on v0

v1 whole, which is shorter than its diff:
```python
from functools import partial

import jax
import jax.numpy as jnp
from jax import lax
from jax.experimental import pallas as pl
from jax.experimental.pallas import tpu as pltpu
from jax.sharding import PartitionSpec as P

C_IN = 128
C_OUT = 256
GROUPS = 32
CPG = 8
TT = 4
TH = 8
TW = 8
TBLK = 6
CLIPS = 3
WBLK = 8
WSLOTS = 16
VOX = 256


epsilon = 1e-05


MESH = pl.DeviceIdType.MESH
TAP = [(a, e, q) for a in range(3) for e in range(3) for q in range(3)]
F32, BF16 = jnp.float32, jnp.bfloat16
ROWS = 27 * C_IN
GVOX = float(VOX * CPG)
SLAB = 60 * 8
VMEM_BYTES = 60 * 1024 * 1024


def remote(src, dst, send, recv, **where):
    return pltpu.make_async_remote_copy(
        src_ref=src, dst_ref=dst, send_sem=send, recv_sem=recv, device_id=where, device_id_type=MESH
    )


def gather_block(block, buf, send, recv, me, count):
    buf[me] = block[...]

    def start(s, c):
        to = lax.rem(me + s, count)
        remote(block, buf.at[me], send.at[s], recv.at[me], tile=to).start()
        return c

    def wait(s, c):
        to = lax.rem(me + s, count)
        remote(block, buf.at[me], send.at[s], recv.at[to], tile=to).wait_send()
        remote(block, buf.at[to], send.at[s], recv.at[to], tile=to).wait_recv()
        return c

    lax.fori_loop(1, count, start, 0)
    lax.fori_loop(1, count, wait, 0)


def shifted(i, x, even, odd):
    for q in range(3):
        y = x[:, :, q : q + 8, :]
        even[q, i] = y.reshape(480, C_IN).astype(BF16)
        odd[q, i] = y[:, 1:9].reshape(384, C_IN).astype(BF16)


def tap_slab(even, odd, i, tap):
    a, e, q = tap
    out = []
    for f in range(TT):
        if e == 1:
            out.append(odd[q, i, pl.ds((f + a) * 64, 64), :])
        else:
            out.append(even[q, i, pl.ds((f + a) * 80 + e * 8, 64), :])
    return jnp.concatenate(out, axis=0)


def pair_slab(even, odd, i, p):
    left = tap_slab(even, odd, i, TAP[p])
    if p + 1 == len(TAP):
        return left
    return jnp.concatenate([left, tap_slab(even, odd, i, TAP[p + 1])], axis=1)


def main_kernel(
    n_tile, n_rep, tiles, filt, up, member, affine, act, grad, norm,
    even, odd, conv, ngrad, cgrad, sums, sq, tmean, tinv, blk, buf, half, other, part, red, zin, zout, fin, nbuf, blk2, buf2,
    g_send, g_recv, h_send, h_recv, c_send, c_recv, p_send, p_recv, z_send, z_recv, y_send, y_recv, f_send, f_recv, n_send, n_recv,
):
    me = lax.axis_index("tile")
    rep = lax.axis_index("rep")
    core = lax.rem(me, 2)
    chip = lax.div(me, 2)
    chips = n_tile // 2
    mate = chip * 2 + 1 - core
    loss_scale = float(n_rep * n_tile * WSLOTS * VOX) ** (-0.5)

    barrier = pltpu.get_barrier_semaphore()

    def greet_tile(s, c):
        pl.semaphore_signal(barrier, inc=1, device_id={"tile": lax.rem(me + s, n_tile)}, device_id_type=MESH)
        return c

    def greet_rep(s, c):
        pl.semaphore_signal(barrier, inc=1, device_id={"rep": lax.rem(rep + s, n_rep)}, device_id_type=MESH)
        return c

    lax.fori_loop(1, n_tile, greet_tile, 0)
    lax.fori_loop(1, n_rep, greet_rep, 0)

    gi = lax.broadcasted_iota(jnp.int32, (C_OUT, C_OUT), 0) >> 3
    gj = lax.broadcasted_iota(jnp.int32, (C_OUT, C_OUT), 1) >> 3
    same_group = (gi == gj).astype(F32)

    def per_group(v):
        return jnp.dot(v, same_group, precision=lax.Precision.HIGHEST, preferred_element_type=F32)

    def forward(n, c):
        for j in range(4):
            shifted(n * 4 + j, tiles[n * 4 + j].astype(F32), even, odd)
        acc = None
        for p in range(0, 27, 2):
            rows = jnp.concatenate([pair_slab(even, odd, n * 4 + j, p) for j in range(4)], axis=0)
            d = jnp.dot(rows, filt[p * C_IN : min(p + 2, 27) * C_IN, :], preferred_element_type=F32)
            acc = d if acc is None else acc + d
        for j in range(4):
            one = acc[j * VOX : (j + 1) * VOX]
            conv[n * 4 + j] = one
            sums[pl.ds(n * 4 + j, 1), :] = jnp.sum(one, axis=0, keepdims=True)
        return c

    lax.fori_loop(0, WSLOTS // 4, forward, 0)

    gsum = per_group(sums[...])
    tmean[...] = gsum / GVOX

    def centre(i, c):
        d = conv[i] - tmean[pl.ds(i, 1), :]
        sq[pl.ds(i, 1), :] = jnp.sum(d * d, axis=0, keepdims=True)
        return c

    lax.fori_loop(0, WSLOTS, centre, 0)
    gsq = per_group(sq[...])
    counts, firsts, seconds = [], [], []
    for k in range(CLIPS):
        m = member[k]
        n_k = jnp.sum(m, axis=0, keepdims=True)
        s_k = jnp.sum(m * gsum, axis=0, keepdims=True)
        mu = s_k / (GVOX * jnp.maximum(n_k, 1.0))
        off = tmean[...] - mu
        counts.append(n_k)
        firsts.append(s_k)
        seconds.append(jnp.sum(m * (gsq + GVOX * off * off), axis=0, keepdims=True))
    blk[...] = jnp.concatenate(counts + firsts + seconds + [jnp.zeros((7, C_OUT), F32)], axis=0)

    pl.semaphore_wait(barrier, n_tile + n_rep - 2)
    gather_block(blk, buf, g_send, g_recv, me, n_tile)

    all_n = buf[:, 0:3, :]
    all_s = buf[:, 3:6, :]
    n_tot = jnp.sum(all_n, axis=0)
    mean = jnp.sum(all_s, axis=0) / (GVOX * n_tot)
    off = all_s / (GVOX * jnp.maximum(all_n, 1.0)) - mean
    var = jnp.sum(buf[:, 6:9, :] + GVOX * all_n * off * off, axis=0) / (GVOX * n_tot)
    inv = lax.rsqrt(var + epsilon)
    tmean[...] = sum(member[k] * mean[k : k + 1] for k in range(CLIPS))
    tinv[...] = sum(member[k] * inv[k : k + 1] for k in range(CLIPS))

    gain = affine[0:1, :]
    shift = affine[1:2, :]

    def middle(i, c):
        mu = tmean[pl.ds(i, 1), :]
        iv = tinv[pl.ds(i, 1), :]
        first = jnp.zeros((1, C_OUT), F32)
        cross = jnp.zeros((1, C_OUT), F32)
        for r in range(0, VOX, 64):
            normed = (conv[i, r : r + 64, :] - mu) * iv
            pre = normed * gain + shift
            sg = 1.0 / (1.0 + jnp.exp(-pre))
            act[i, r : r + 64, :] = (pre * sg).astype(BF16)
            pg = (up[i, r : r + 64, :].astype(F32) * loss_scale) * sg * (1.0 + pre * (1.0 - sg))
            first += jnp.sum(pg, axis=0, keepdims=True)
            cross += jnp.sum(pg * normed, axis=0, keepdims=True)
            conv[i, r : r + 64, :] = normed
            ngrad[i, r : r + 64, :] = pg * gain
        sums[pl.ds(i, 1), :] = first
        sq[pl.ds(i, 1), :] = cross
        return c

    lax.fori_loop(0, WSLOTS, middle, 0)
    firsts = [jnp.sum(member[k] * sums[...], axis=0, keepdims=True) for k in range(CLIPS)]
    crosses = [jnp.sum(member[k] * sq[...], axis=0, keepdims=True) for k in range(CLIPS)]
    blk2[...] = jnp.concatenate(firsts + crosses + [jnp.zeros((2, C_OUT), F32)], axis=0)
    gather_block(blk2, buf2, h_send, h_recv, me, n_tile)
    total = jnp.sum(buf2[...], axis=0)

    both = jnp.concatenate(
        [jnp.sum(total[3:6], axis=0, keepdims=True), jnp.sum(total[0:3], axis=0, keepdims=True), jnp.zeros((6, C_OUT), F32)], axis=0
    )
    nbuf[rep] = both

    def norm_start(s, c):
        to = lax.rem(rep + s, n_rep)
        remote(nbuf.at[rep], nbuf.at[rep], n_send.at[s], n_recv.at[rep], rep=to).start()
        return c

    def norm_wait(s, c):
        to = lax.rem(rep + s, n_rep)
        remote(nbuf.at[rep], nbuf.at[rep], n_send.at[s], n_recv.at[to], rep=to).wait_send()
        remote(nbuf.at[rep], nbuf.at[to], n_send.at[s], n_recv.at[to], rep=to).wait_recv()
        return c

    lax.fori_loop(1, n_rep, norm_start, 0)

    scaled = per_group(total * gain)
    spread_n = GVOX * n_tot
    mg = scaled[0:3] / spread_n
    mc = scaled[3:6] / spread_n
    sums[...] = sum(member[k] * mg[k : k + 1] for k in range(CLIPS))
    sq[...] = sum(member[k] * mc[k : k + 1] for k in range(CLIPS))

    def conv_gradient(i, c):
        iv = tinv[pl.ds(i, 1), :]
        m1 = sums[pl.ds(i, 1), :]
        m2 = sq[pl.ds(i, 1), :]
        for r in range(0, VOX, 64):
            g = iv * (ngrad[i, r : r + 64, :] - m1 - conv[i, r : r + 64, :] * m2)
            cgrad[i, r : r + 64, :] = g.astype(BF16)
        return c

    lax.fori_loop(0, WSLOTS, conv_gradient, 0)

    share = ROWS // chips

    def mate_copy(p):
        rows = pl.ds(p * C_IN, (min(p + 2, 27) - p) * C_IN)
        return remote(half.at[1 - core, rows], other.at[rows], c_send.at[p // 2], c_recv.at[p // 2], tile=mate)

    def chip_copy(j, k):
        return remote(half.at[core, pl.ds(j * share, share)], part.at[k], p_send.at[j], p_recv.at[k], tile=j * 2 + core)

    done = [0]

    def settle(p):
        lo, hi = p * C_IN, min(p + 2, 27) * C_IN
        mate_copy(p).wait_recv()
        half[core, lo:hi, :] = half[core, lo:hi, :] + other[lo:hi, :]
        while (done[0] + 1) * share <= hi:
            j = done[0]

            @pl.when(chip != j)
            def _():
                chip_copy(j, chip).start()

            @pl.when(chip == j)
            def _():
                part[j] = half[core, j * share : (j + 1) * share, :]

            done[0] += 1

    lag = 4
    for p in range(0, 27, 2):
        d = None
        for u in range(0, WSLOTS, 4):
            rows = jnp.concatenate([pair_slab(even, odd, i, p) for i in range(u, u + 4)], axis=0)
            g = jnp.concatenate([cgrad[i] for i in range(u, u + 4)], axis=0)
            t = lax.dot_general(rows, g, (((0,), (0,)), ((), ())), preferred_element_type=F32)
            d = t if d is None else d + t
        lo, hi = p * C_IN, min(p + 2, 27) * C_IN
        half[0, lo:hi, :] = d[:, :128]
        half[1, lo:hi, :] = d[:, 128:]
        mate_copy(p).start()
        if p >= lag:
            settle(p - lag)
    for p in range(0, 27, 2):
        if p + lag >= 27:
            settle(p)

    def plane_wait(s, c):
        j = lax.rem(chip + s, chips)
        chip_copy(j, chip).wait_send()
        chip_copy(j, j).wait_recv()
        return c

    lax.fori_loop(1, chips, plane_wait, 0)
    for p in range(0, 27, 2):
        mate_copy(p).wait_send()

    piece = red.shape[0] // n_rep
    red[0:share, :] = jnp.sum(part[...], axis=0)
    if red.shape[0] > share:
        red[share:, :] = jnp.zeros((red.shape[0] - share, 128), F32)
    zin[rep] = red[pl.ds(pl.multiple_of(rep * piece, 8), piece), :]

    def z_copy(to, slot, s):
        return remote(red.at[pl.ds(pl.multiple_of(to * piece, 8), piece)], zin.at[slot], z_send.at[s], z_recv.at[slot], rep=to)

    def y_copy(to, slot, s):
        rows = pl.ds(pl.multiple_of(slot * piece, 8), piece)
        mine = pl.ds(pl.multiple_of(rep * piece, 8), piece)
        return remote(zout.at[mine], zout.at[rows], y_send.at[s], y_recv.at[slot], rep=to)

    def each(what):
        def body(s, c):
            what(lax.rem(rep + s, n_rep), s)
            return c

        lax.fori_loop(1, n_rep, body, 0)

    each(lambda to, s: z_copy(to, rep, s).start())
    lax.fori_loop(1, n_rep, norm_wait, 0)
    norm[...] = jnp.sum(nbuf[...], axis=0)
    each(lambda to, s: z_copy(to, rep, s).wait_send())
    each(lambda to, s: z_copy(to, to, s).wait_recv())
    zout[pl.ds(pl.multiple_of(rep * piece, 8), piece), :] = jnp.sum(zin[...], axis=0)
    each(lambda to, s: y_copy(to, rep, s).start())
    each(lambda to, s: y_copy(to, rep, s).wait_send())
    each(lambda to, s: y_copy(to, to, s).wait_recv())

    keep = grad.shape[0]
    skip = share - keep

    def rows_of(c):
        return pl.ds(pl.multiple_of(c * skip, 8), keep)

    swap = remote(zout.at[rows_of(1 - core)], fin, f_send, f_recv, tile=mate)
    swap.start()
    swap.wait()
    own = zout[rows_of(core), :]
    there = fin[...]
    grad[:, 0:128] = jnp.where(core == 0, own, there)
    grad[:, 128:256] = jnp.where(core == 0, there, own)


def main_call(n_tile, n_rep, tiles, filt, up, member, affine):
    chips = n_tile // 2
    share = ROWS // chips
    keep = share // 2 + 4 if (share // 2) % 8 else share // 2
    padded = -(-share // (8 * n_rep)) * 8 * n_rep
    whole = pl.BlockSpec(memory_space=pltpu.VMEM)
    dma = pltpu.SemaphoreType.DMA
    return pl.pallas_call(
        partial(main_kernel, n_tile, n_rep),
        out_shape=(
            jax.ShapeDtypeStruct((WSLOTS, VOX, C_OUT), BF16),
            jax.ShapeDtypeStruct((keep, C_OUT), F32),
            jax.ShapeDtypeStruct((8, C_OUT), F32),
        ),
        in_specs=[whole] * 5,
        out_specs=(whole,) * 3,
        scratch_shapes=[
            pltpu.VMEM((3, WSLOTS, 480, C_IN), BF16),
            pltpu.VMEM((3, WSLOTS, 384, C_IN), BF16),
            pltpu.VMEM((WSLOTS, VOX, C_OUT), F32),
            pltpu.VMEM((WSLOTS, VOX, C_OUT), F32),
            pltpu.VMEM((WSLOTS, VOX, C_OUT), BF16),
            pltpu.VMEM((WSLOTS, C_OUT), F32),
            pltpu.VMEM((WSLOTS, C_OUT), F32),
            pltpu.VMEM((WSLOTS, C_OUT), F32),
            pltpu.VMEM((WSLOTS, C_OUT), F32),
            pltpu.VMEM((16, C_OUT), F32),
            pltpu.VMEM((n_tile, 16, C_OUT), F32),
            pltpu.VMEM((2, ROWS, 128), F32),
            pltpu.VMEM((ROWS, 128), F32),
            pltpu.VMEM((chips, share, 128), F32),
            pltpu.VMEM((padded, 128), F32),
            pltpu.VMEM((n_rep, padded // n_rep, 128), F32),
            pltpu.VMEM((padded, 128), F32),
            pltpu.VMEM((keep, 128), F32),
            pltpu.VMEM((n_rep, 8, C_OUT), F32),
            pltpu.VMEM((8, C_OUT), F32),
            pltpu.VMEM((n_tile, 8, C_OUT), F32),
        ]
        + [dma((n_tile,))] * 4
        + [dma((14,))] * 2
        + [dma((chips,))] * 2
        + [dma((n_rep,))] * 4
        + [dma] * 2
        + [dma((n_rep,))] * 2,
        compiler_params=pltpu.CompilerParams(collective_id=0, has_side_effects=True, vmem_limit_bytes=VMEM_BYTES),
        cost_estimate=pl.CostEstimate(flops=4 * WSLOTS * VOX * ROWS * C_OUT, bytes_accessed=16 * 1024 * 1024, transcendentals=WSLOTS * VOX * C_OUT),
        name="conv_norm",
    )(tiles, filt, up, member, affine)


def extended(cells, sides, width):
    for axis, dim in sides:
        count = lax.axis_size(axis)
        ends = count - 1
        head = lax.slice_in_dim(cells, 0, width, axis=dim)
        tail = lax.slice_in_dim(cells, cells.shape[dim] - width, cells.shape[dim], axis=dim)
        cells = jnp.concatenate(
            [
                lax.ppermute(tail, axis, [(i, (i + 1) % count) for i in range(ends)]),
                cells,
                lax.ppermute(head, axis, [((i + 1) % count, i) for i in range(ends)]),
            ],
            axis=dim,
        )
    return cells


def cut_tile(padded, clip_ids, strip_row, slot_id):
    block_id = slot_id // WBLK
    width_block = slot_id % WBLK
    zero_start = jnp.zeros((), jnp.int32)
    section = lax.dynamic_slice(
        padded,
        (block_id * TT, strip_row, width_block * TW, zero_start),
        (TT + 2, TH + 2, TW + 2, C_IN),
    )
    earlier = clip_ids[jnp.maximum(block_id - 1, 0)]
    linked = jnp.logical_and(block_id > 0, earlier == clip_ids[block_id])
    history = jnp.where(linked, section[:2], jnp.zeros_like(section[:2]))
    return jnp.concatenate([history, section[2:]], axis=0)


def shards(
    input_video,
    block_clip,
    send_slot,
    recv_index,
    tile_clip,
    kernel,
    norm_gain,
    norm_shift,
    upstream,
):
    peer_count = lax.axis_size("tile")
    frames = input_video[0]
    clip_ids = block_clip[0]
    rimmed = extended(frames, (("tile", 1),), 1)
    padded = jnp.pad(rimmed, ((2, 0), (0, 0), (1, 1), (0, 0)))
    send_plan = send_slot[0, 0]
    capacity = send_plan.shape[1]
    chosen = jnp.minimum(send_plan.reshape(-1), TBLK * WBLK - 1)
    zero_rows = jnp.zeros_like(chosen)
    outgoing = jax.vmap(partial(cut_tile, padded, clip_ids))(zero_rows, chosen)
    outgoing = outgoing.reshape((peer_count, capacity) + outgoing.shape[1:])
    arrived = lax.all_to_all(outgoing, "tile", split_axis=0, concat_axis=0, tiled=True)
    arrived = arrived.reshape((peer_count * capacity,) + arrived.shape[2:])
    work_tiles = arrived[recv_index[0, 0]]

    clips = jnp.arange(CLIPS, dtype=jnp.int32)[:, None, None]
    member = jnp.broadcast_to((tile_clip[0, 0][None, :, None] == clips).astype(F32), (CLIPS, WSLOTS, C_OUT))
    affine = jnp.concatenate([norm_gain[None], norm_shift[None], jnp.zeros((6, C_OUT), F32)], axis=0)
    activation, grad_rows, norm_rows = main_call(
        peer_count, lax.axis_size("rep"), work_tiles, kernel, upstream[0, 0], member, affine
    )
    row_share = ROWS // peer_count
    skip = (grad_rows.shape[0] - row_share) * lax.rem(lax.axis_index("tile"), 2)
    grad_shard = lax.dynamic_slice_in_dim(grad_rows, skip, row_share, 0)
    return (activation[None, None], grad_shard, norm_rows[:2])


def solution(mesh):
    placed = (
        P("rep", None, "tile", None, None),
        P("rep", None),
        P("rep", "tile", None, None),
        P("rep", "tile", None),
        P("rep", "tile", None),
        P(),
        P(),
        P(),
        P("rep", "tile", None, None, None),
    )
    return jax.shard_map(
        shards,
        mesh=mesh,
        in_specs=placed,
        out_specs=(P("rep", "tile", None, None, None), P("tile", None), P()),
        check_vma=False,
    )
```

time: 2200 us -> 323 us (0.15); the launches traced: 2170 us -> 320 us
  local copies, waits for them, and re-layouts: 1410 us -> 71.1 us
  blocking collectives: 272 us -> 0 us
  waiting for transfers between devices: 306 us -> 118 us
  matrix products: 102 us -> 0 us
  Pallas kernels: 0 us -> 91.8 us
  other arithmetic: 48.3 us -> 25 us
    while x865 -> x0, local copies, waits for them, and re-layouts: 1280 us -> none
    psum x4 -> x0, blocking collectives: 272 us -> none  [the longest x1 94.3 us: shards(): lax.psum((kernel_local, norm_local), ('tile', 'rep'))]
    psum x1 -> x0, waiting for transfers between devices: 188 us -> none  [shards(): lax.psum((kernel_local, norm_local), ('tile', 'rep'))]
    dot_general x40 -> x0, matrix products: 102 us -> none  [the longest x16 48.2 us: add_whole(): lax.dot_general(unfold(one_tile[None]), tile_grad, (((0,), (0,)), ((), ()...]
    pallas_call x0 -> x1, Pallas kernels: none -> 91.8 us  [main_call(): pl.pallas_call(partial(main_kernel, n_tile, n_rep), out_shape=(jax.ShapeD...]
    another operation x32 -> x0, local copies, waits for them, and re-layouts: 50.1 us -> none  [unfold(): return jnp.stack(columns, axis=4).reshape(-1, 27 * tile_stack.shape[-1])]
  transfers between devices with their start and end apart: 4 -> 3, of which waited for: 2 -> 1; matrix products, arithmetic and copies ran while one was open for 0% -> 3% of each run, Pallas kernels for 0% -> 0%
where the time goes in v1:
time: 323 us; the launch traced here: 320 us
  waiting for transfers between devices  118 us (37%)
  Pallas kernels  91.8 us (28%)
  local copies, waits for them, and re-layouts  71.1 us (22%)
  other arithmetic  25 us (8%)
  starting transfers between devices  13.5 us (4%)
    all_to_all x1, waiting for transfers between devices, shards(): lax.all_to_all(outgoing, 'tile', split_axis=0, concat_axis=0, tiled=True)  118 us
    pallas_call x1, Pallas kernels, main_call(): pl.pallas_call(partial(main_kernel, n_tile, n_rep), out_shape=(jax.ShapeD...  91.8 us
    reshape x1, local copies, waits for them, and re-layouts, shards(): outgoing = outgoing.reshape((peer_count, capacity) + outgoing.shape[1:])  18 us
    all_to_all x1, local copies, waits for them, and re-layouts, shards(): lax.all_to_all(outgoing, 'tile', split_axis=0, concat_axis=0, tiled=True)  11.3 us
    concatenate x1, other arithmetic, extended(): jnp.concatenate([lax.ppermute(tail, axis, [(i, (i + 1) % count) for i in...  10.2 us
    gather x1, local copies, waits for them, and re-layouts, cut_tile(): lax.dynamic_slice(padded, (block_id * TT, strip_row, width_block * TW, ze...  10.2 us
    gather x2, local copies, waits for them, and re-layouts, shards(): work_tiles = arrived[recv_index[0, 0]]  8.59 us
    unnamed x14, local copies, waits for them, and re-layouts  7.87 us
  transfers between devices with their start and end apart: 3, of which 1 were waited for; matrix products, arithmetic and copies ran while one was open for 3% of the time, Pallas kernels for 0%

profile of v1, /device:TPU:24, one launch (start us, length us, event | category | flops | bytes accessed | tf_op | source)
XLA Modules:
  0.0 320.0 jit_solution(164707686351975941)
XLA Ops:
  0.6 0.0 copy-start.1
  0.6 0.0 copy-start
  0.7 4.7 %copy.31 = bf16[1,24,8,64,128]{4,2,3,1,0:T(8,128)(2,1)S(1)} copy(bf16[1,24,8,64,128]{4,3,2,1,0:T(8,128)(2,1)} %param.9) | data formatting | bytes 6291456 | tf_op args[0]
  5.4 1.7 fusion.19
  7.1 0.1 copy.23
  7.2 1.9 collective-permute-start
  9.1 0.8 copy.24
  9.9 5.7 %collective-permute-start.1 = (bf16[24,1,64,128]{3,2,1,0:T(8,128)(2,1)}, bf16[24,1,64,128]{3,2,1,0:T(8,128)(2,1)}, u32[]{:S(2)}, u32[]{:S(2)}) collective-permute-start(bf16[24,1,64,128]{3,2,1,0:T(8,128)(2,1)} %copy.24), channel_id=1, source_target_pairs={{8,0},{16,8},{24,16},{32,24},{40,32},{48,40},{56,48},{64,56},{72,6... | collective-permute-start | bytes 1179656 | tf_op jit(solution)/shard_map/ppermute | solution.py:397
  15.6 0.0 copy-done.1
  15.7 0.7 copy.20
  16.4 0.8 min.34
  17.2 0.8 min.33
  18.0 0.0 copy-done
  18.0 0.7 fusion.20
  18.7 3.8 %bitcast_and_fusion = (pred[64]{0:T(512)(128)(4,1)S(1)}, s32[64,1]{0,1:T(1,128)S(1)}) fusion(s32[64]{0:T(128)S(1)} %min.33, s32[]{:T(128)} %bitcast, s32[]{:T(128)} %bitcast.1, s32[]{:T(128)} %bitcast.2, s32[]{:T(128)} %bitcast.3, s32[]{:T(128)} %bitcast.5, s32[]{:T(128)} %bitcast.4, s32[64,1]{0,1:T(1,128)S(1)} %min.34), kind=kLoop, calls=%fused_computation.26 | loop fusion | flops 3712 | bytes 856 | tf_op jit(solution)/shard_map/vmap()/and | solution.py:414
  22.5 0.0 collective-permute-done
  22.5 1.8 copy.25
  24.3 0.0 collective-permute-done.1
  24.3 1.8 copy.26
  26.1 10.2 %fusion.7 = bf16[26,10,66,128]{3,1,2,0:T(8,128)(2,1)} fusion(bf16[24,1,64,128]{3,1,2,0:T(2,128)(2,1)S(1)} %copy.26, bf16[24,8,64,128]{3,1,2,0:T(8,128)(2,1)S(1)} %bitcast.31, bf16[24,1,64,128]{3,1,2,0:T(2,128)(2,1)S(1)} %copy.25), kind=kLoop, calls=%fused_computation.13 | loop fusion | flops 37340160 | bytes 8325120 | tf_op jit(solution)/shard_map/concatenate | solution.py:393
  36.4 10.2 %gather_fusion = bf16[64,6,10,10,128]{4,2,3,1,0:T(8,128)(2,1)} fusion(bf16[26,10,66,128]{3,1,2,0:T(8,128)(2,1)} %fusion.7, s32[64]{0:T(128)S(1)} %fusion.18), kind=kCustom, calls=%fused_computation | custom fusion | bytes 19661824 | tf_op jit(solution)/shard_map/vmap()/gather | solution.py:408
  46.5 0.0 slice-start
  46.6 3.1 slice_select_fusion
  49.6 2.5 slice-done
  52.1 7.2 %pad_maximum_fusion = bf16[64,6,10,10,128]{4,2,3,1,0:T(8,128)(2,1)} fusion(bf16[64,4,10,10,128]{4,2,3,1,0:T(8,128)(2,1)S(1)} %slice-done, bf16[64,2,10,10,128]{4,2,3,1,0:T(8,128)(2,1)S(1)} %slice_select_fusion), kind=kLoop, calls=%fused_computation.4 | loop fusion | flops 4915200 | bytes 19660800 | tf_op jit(solution)/shard_map/vmap()/concatenate | solution.py:416
  59.3 18.0 %copy.27 = bf16[32,2,6,10,10,128]{5,1,4,3,2,0:T(2,128)(2,1)} copy(bf16[32,2,6,10,10,128]{5,3,4,2,1,0:T(8,128)(2,1)} %bitcast.28) | data formatting | bytes 19660800 | tf_op jit(solution)/shard_map/reshape | solution.py:440
  77.2 0.0 copy-start.5
  77.2 0.0 copy-start.4
  77.3 0.0 copy-start.2
  77.3 0.0 copy-start.3
  77.3 5.8 %all-to-all-start = ((bf16[32,2,6,10,10,128]{5,1,4,3,2,0:T(2,128)(2,1)}), bf16[32,2,6,10,10,128]{5,1,4,3,2,0:T(2,128)(2,1)}, u32[]{:S(2)}, u32[]{:S(2)}) async-start(bf16[32,2,6,10,10,128]{5,1,4,3,2,0:T(2,128)(2,1)} %copy.27), calls=%async_computation | async-start | bytes 19660800 | tf_op jit(solution)/shard_map/all_to_all | solution.py:441
  83.1 0.1 pad.7.clone
  83.2 0.0 copy-done.5
  83.2 0.0 copy-done.4
  83.3 0.0 copy-done.2
  83.3 0.0 copy-done.3
  83.3 0.7 maximum_maximum_fusion.affine
  83.9 117.8 %all-to-all-done = bf16[32,2,6,10,10,128]{5,1,4,3,2,0:T(2,128)(2,1)} async-done(((bf16[32,2,6,10,10,128]{5,1,4,3,2,0:T(2,128)(2,1)}), bf16[32,2,6,10,10,128]{5,1,4,3,2,0:T(2,128)(2,1)}, u32[]{:S(2)}, u32[]{:S(2)}) %all-to-all-start) | async-done | bytes 9830432 | tf_op jit(solution)/shard_map/all_to_all | solution.py:441
  201.7 11.3 %copy.28 = bf16[32,2,6,10,10,128]{5,2,4,3,1,0:T(8,128)(2,1)} copy(bf16[32,2,6,10,10,128]{5,1,4,3,2,0:T(2,128)(2,1)} %all-to-all-done) | data formatting | bytes 19660800 | tf_op jit(solution)/shard_map/all_to_all | solution.py:441
  213.0 5.9 %gather_fusion.1 = bf16[16,6,10,10,128]{4,1,3,2,0:T(8,128)(2,1)S(1)} fusion(bf16[64,6,10,10,128]{4,1,3,2,0:T(8,128)(2,1)} %bitcast.29, s32[1024]{0:T(1024)S(1)} %pad_clamp_fusion), kind=kCustom, calls=%fused_computation.1 | custom fusion | bytes 4915264 | tf_op jit(solution)/shard_map/gather | solution.py:443
  218.9 2.7 copy.29.tiles
  221.6 0.7 broadcast_in_dim.34.member
  222.3 91.8 %conv_norm.1 = (bf16[16,256,256]{2,1,0:T(8,128)(2,1)}, f32[112,256]{1,0:T(8,128)}, f32[8,256]{1,0:T(8,128)}) custom-call(bf16[16,6,10,10,128]{4,3,2,1,0:T(8,128)(2,1)} %copy.29.tiles, bf16[3456,256]{1,0:T(8,128)(2,1)} %filt.1, bf16[16,256,256]{2,1,0:T(8,128)(2,1)} %bitcast.36, f32[3,16,256]{2,1,0:T(8,128)} %broadcast_in_dim.34.member, ...), custom_call_target="tpu_custom_call" | custom-call | flops 14495514624 | bytes 16777216 | tf_op jit(solution)/shard_map/conv_norm/pallas_call | solution.py:343
  314.1 1.3 slice.19
  315.4 1.6 constant_dynamic-slice_fusion
  316.9 3.1 copy.33
  (6 shorter events, 0.0 us)
Async XLA Ops:
  0.6 15.0 %copy-start.1 = (s32[1,1,32,2]{2,3,1,0:T(2,128)S(1)}, s32[1,1,32,2]{2,3,1,0:T(2,128)}, u32[]{:S(2)}) copy-start(s32[1,1,32,2]{2,3,1,0:T(2,128)} %param.11) | copy-start | bytes 772
  0.6 17.4 %copy-start = (s32[1,6]{1,0:T(1,128)S(1)}, s32[1,6]{1,0:T(1,128)}, u32[]{:S(2)}) copy-start(s32[1,6]{1,0:T(1,128)} %param.10) | copy-start | bytes 76
  7.2 15.4 %collective-permute-start = (bf16[24,1,64,128]{3,2,1,0:T(8,128)(2,1)S(1)}, bf16[24,1,64,128]{3,2,1,0:T(8,128)(2,1)}, u32[]{:S(2)}, u32[]{:S(2)}) collective-permute-start(bf16[24,1,64,128]{3,2,1,0:T(8,128)(2,1)S(1)} %copy.23), channel_id=1, source_target_pairs={{0,8},{8,16},{16,24},{24,32},{32,40},{40,48},{48,56},{56,64},{64,7... | collective-permute-start | bytes 1179656 | tf_op jit(solution)/shard_map/ppermute | solution.py:395
  9.9 14.4 %collective-permute-start.1 = (bf16[24,1,64,128]{3,2,1,0:T(8,128)(2,1)}, bf16[24,1,64,128]{3,2,1,0:T(8,128)(2,1)}, u32[]{:S(2)}, u32[]{:S(2)}) collective-permute-start(bf16[24,1,64,128]{3,2,1,0:T(8,128)(2,1)} %copy.24), channel_id=1, source_target_pairs={{8,0},{16,8},{24,16},{32,24},{40,32},{48,40},{56,48},{64,56},{72,6... | collective-permute-start | bytes 1179656 | tf_op jit(solution)/shard_map/ppermute | solution.py:397
  46.5 5.5 %slice-start = ((bf16[64,6,10,10,128]{4,2,3,1,0:T(8,128)(2,1)}), bf16[64,4,10,10,128]{4,2,3,1,0:T(8,128)(2,1)S(1)}, s32[]{:S(2)}) async-start(bf16[64,6,10,10,128]{4,2,3,1,0:T(8,128)(2,1)} %gather_fusion), calls=%async_computation.1 | async-start | bytes 20971520 | tf_op jit(solution)/shard_map/vmap()/slice | solution.py:416
  77.2 6.0 %copy-start.5 = (s32[1,1,16]{2,1,0:T(1,128)S(1)}, s32[1,1,16]{2,1,0:T(1,128)}, u32[]{:S(2)}) copy-start(s32[1,1,16]{2,1,0:T(1,128)} %param.12) | copy-start | bytes 196
  77.2 6.0 %copy-start.4 = (s32[1,1,16]{2,1,0:T(1,128)S(1)}, s32[1,1,16]{2,1,0:T(1,128)}, u32[]{:S(2)}) copy-start(s32[1,1,16]{2,1,0:T(1,128)} %param.13) | copy-start | bytes 196
  77.3 6.0 %copy-start.2 = (f32[256]{0:T(256)S(1)}, f32[256]{0:T(256)}, u32[]{:S(2)}) copy-start(f32[256]{0:T(256)} %param.16) | copy-start | bytes 3076
  77.3 6.0 %copy-start.3 = (f32[256]{0:T(256)S(1)}, f32[256]{0:T(256)}, u32[]{:S(2)}) copy-start(f32[256]{0:T(256)} %param.15) | copy-start | bytes 3076
  77.3 124.4 %all-to-all-start = ((bf16[32,2,6,10,10,128]{5,1,4,3,2,0:T(2,128)(2,1)}), bf16[32,2,6,10,10,128]{5,1,4,3,2,0:T(2,128)(2,1)}, u32[]{:S(2)}, u32[]{:S(2)}) async-start(bf16[32,2,6,10,10,128]{5,1,4,3,2,0:T(2,128)(2,1)} %copy.27), calls=%async_computation | async-start | bytes 19660800 | tf_op jit(solution)/shard_map/all_to_all | solution.py:441

commit v2 on v1

--- a/solution.py
+++ b/solution.py
@@ -19,6 +19,7 @@
 WBLK = 8
 WSLOTS = 16
 VOX = 256
+FRAMES = 24
 
 
 epsilon = 1e-05
@@ -384,36 +385,224 @@
     )(tiles, filt, up, member, affine)
 
 
-def extended(cells, sides, width):
-    for axis, dim in sides:
-        count = lax.axis_size(axis)
-        ends = count - 1
-        head = lax.slice_in_dim(cells, 0, width, axis=dim)
-        tail = lax.slice_in_dim(cells, cells.shape[dim] - width, cells.shape[dim], axis=dim)
-        cells = jnp.concatenate(
-            [
-                lax.ppermute(tail, axis, [(i, (i + 1) % count) for i in range(ends)]),
-                cells,
-                lax.ppermute(head, axis, [((i + 1) % count, i) for i in range(ends)]),
-            ],
-            axis=dim,
-        )
-    return cells
-
-
-def cut_tile(padded, clip_ids, strip_row, slot_id):
-    block_id = slot_id // WBLK
-    width_block = slot_id % WBLK
-    zero_start = jnp.zeros((), jnp.int32)
-    section = lax.dynamic_slice(
-        padded,
-        (block_id * TT, strip_row, width_block * TW, zero_start),
-        (TT + 2, TH + 2, TW + 2, C_IN),
-    )
-    earlier = clip_ids[jnp.maximum(block_id - 1, 0)]
-    linked = jnp.logical_and(block_id > 0, earlier == clip_ids[block_id])
-    history = jnp.where(linked, section[:2], jnp.zeros_like(section[:2]))
-    return jnp.concatenate([history, section[2:]], axis=0)
+FMOD = 6
+RMOD = 5
+STOPS = FMOD * RMOD
+PIECE = 20
+PLANES = FRAMES // FMOD
+
+
+def exchange_kernel(
+    n_tile, lines, strip, mine, meta, tiles,
+    tab, stab, raw, wide, stage, sendb, recvb, rows32,
+    t_send, t_recv, s_sem, v_send, v_recv, v_own, w_send, w_recv,
+):
+    me = lax.axis_index("tile")
+    my_f = lax.rem(me, FMOD)
+    my_r = lax.div(me, FMOD)
+    depth = lines // RMOD + 2
+
+    barrier = pltpu.get_barrier_semaphore()
+
+    def greet(s, c):
+        pl.semaphore_signal(barrier, inc=1, device_id={"tile": lax.rem(me + s, n_tile)}, device_id_type=MESH)
+        return c
+
+    lax.fori_loop(1, n_tile, greet, 0)
+    tab[me] = mine[...]
+    pl.semaphore_wait(barrier, n_tile - 1)
+
+    def table(to, slot, s):
+        return remote(mine, tab.at[slot], t_send.at[s], t_recv.at[slot], tile=to)
+
+    def table_start(s, c):
+        table(lax.rem(me + s, n_tile), me, s).start()
+        return c
+
+    def table_wait(s, c):
+        to = lax.rem(me + s, n_tile)
+        table(to, me, s).wait_send()
+        table(to, to, s).wait_recv()
+        return c
+
+    lax.fori_loop(1, n_tile, table_start, 0)
+
+    def line(h):
+        y = me * TH + h
+        return lax.rem(y, RMOD) * FMOD, lax.div(y, RMOD)
+
+    def spread(n, c):
+        h = lax.div(n, FMOD)
+        a = lax.rem(n + me, FMOD)
+        stop, index = line(h)
+        to = stop + a
+
+        @pl.when(to != me)
+        def _():
+            remote(strip.at[:, a, h], raw.at[:, index], v_send.at[n], v_recv.at[index], tile=to).start()
+
+        @pl.when(to == me)
+        def _():
+            pltpu.make_async_copy(strip.at[:, a, h], raw.at[:, index], v_own.at[h]).start()
+
+        return c
+
+    lax.fori_loop(0, TH * FMOD, spread, 0)
+
+    def clear(i, c):
+        wide[i] = jnp.zeros(wide.shape[1:], F32)
+        return c
+
+    lax.fori_loop(0, wide.shape[0], clear, 0)
+
+    lax.fori_loop(1, n_tile, table_wait, 0)
+    scalars = pltpu.make_async_copy(tab, stab, s_sem)
+    scalars.start()
+
+    @pl.when(me < STOPS)
+    def _():
+        def arrive(i, c):
+            y = i * RMOD + my_r
+            owner = lax.div(y, TH)
+            h = lax.rem(y, TH)
+
+            @pl.when(owner != me)
+            def _():
+                remote(strip.at[:, my_f, h], raw.at[:, i], v_send.at[0], v_recv.at[i], tile=owner).wait_recv()
+
+            @pl.when(owner == me)
+            def _():
+                pltpu.make_async_copy(strip.at[:, my_f, h], raw.at[:, i], v_own.at[h]).wait()
+
+            for k in range(PLANES):
+                line = raw[k, i].astype(F32)
+                gap = jnp.zeros((1, C_IN), F32)
+                line = jnp.concatenate([gap, line, gap, jnp.zeros((6, C_IN), F32)], axis=0)
+                wide[k * depth + i + 1] = line.reshape(WBLK + 1, 8, C_IN)
+            return c
+
+        lax.fori_loop(0, lax.div(lines - my_r + RMOD - 1, RMOD), arrive, 0)
+
+    scalars.wait()
+
+    @pl.when(me < STOPS)
+    def _():
+        def serve(s, c):
+            w = lax.rem(me + s, n_tile)
+            for j in range(WSLOTS):
+                r = stab[w, 0, 64 + j]
+                t = lax.div(r, 2)
+                slot = stab[t, 0, w * 2 + lax.rem(r, 2)]
+                base = meta[0, lax.div(slot, WBLK)] + meta[0, 8 + t]
+                first = lax.rem(slot, WBLK)
+                for half in range(2):
+                    at = j * PIECE + half * 10
+                    stage[at : at + 8, :] = wide[base + half, first]
+                    stage[at + 8 : at + 10, :] = wide[base + half, first + 1][:2]
+            sendb[w] = stage[...].astype(BF16)
+
+            @pl.when(w != me)
+            def _():
+                remote(sendb.at[w], recvb.at[me], w_send.at[w], w_recv.at[me], tile=w).start()
+
+            @pl.when(w == me)
+            def _():
+                recvb[me] = sendb[me]
+
+            return c
+
+        lax.fori_loop(1, n_tile + 1, serve, 0)
+
+    def land(s, c):
+        i = lax.rem(me + n_tile - s, n_tile)
+
+        @pl.when(i < STOPS)
+        def _():
+            @pl.when(i != me)
+            def _():
+                remote(sendb.at[0], recvb.at[i], w_send.at[0], w_recv.at[i], tile=i).wait_recv()
+
+            v = recvb[i].astype(F32)
+            for j in range(WSLOTS):
+                for half in range(2):
+                    at = j * PIECE + half * 10
+                    rows32[i * 2 * WSLOTS + j * 2 + half, 0:10, :] = v[at : at + 10]
+
+        return c
+
+    lax.fori_loop(1, n_tile + 1, land, 0)
+
+    def build(j, c):
+        r = stab[me, 0, 64 + j]
+        t = lax.div(r, 2)
+        b = lax.div(stab[t, 0, me * 2 + lax.rem(r, 2)], WBLK)
+        for f in range(TT + 2):
+            a = lax.rem(b * TT + TT + f, FMOD)
+            for y in range(RMOD):
+                q = lax.rem(t * TH + 4 + y, RMOD)
+                at = (q * FMOD + a) * (2 * WSLOTS) + j * 2
+                for half in range(2):
+                    tiles[j, f, y + half * RMOD] = rows32[at + half, 0:10, :].astype(BF16)
+        return c
+
+    lax.fori_loop(0, WSLOTS, build, 0)
+
+    def sent(n, c):
+        h = lax.div(n, FMOD)
+        a = lax.rem(n + me, FMOD)
+        stop, index = line(h)
+        to = stop + a
+
+        @pl.when(to != me)
+        def _():
+            remote(strip.at[:, a, h], raw.at[:, index], v_send.at[n], v_recv.at[index], tile=to).wait_send()
+
+        return c
+
+    lax.fori_loop(0, TH * FMOD, sent, 0)
+
+    @pl.when(me < STOPS)
+    def _():
+        def served(s, c):
+            w = lax.rem(me + s, n_tile)
+            remote(sendb.at[w], recvb.at[me], w_send.at[w], w_recv.at[me], tile=w).wait_send()
+            return c
+
+        lax.fori_loop(1, n_tile, served, 0)
+
+
+def exchange_call(n_tile, strip, mine, meta):
+    lines = n_tile * TH
+    depth = lines // RMOD + 2
+    whole = pl.BlockSpec(memory_space=pltpu.VMEM)
+    dma = pltpu.SemaphoreType.DMA
+    return pl.pallas_call(
+        partial(exchange_kernel, n_tile, lines),
+        out_shape=jax.ShapeDtypeStruct((WSLOTS, TT + 2, TH + 2, TW + 2, C_IN), BF16),
+        in_specs=[pl.BlockSpec(memory_space=pl.ANY), whole, pl.BlockSpec(memory_space=pltpu.SMEM)],
+        out_specs=whole,
+        scratch_shapes=[
+            pltpu.VMEM((n_tile, 1, 128), jnp.int32),
+            pltpu.SMEM((n_tile, 1, 128), jnp.int32),
+            pltpu.VMEM((PLANES, lines // RMOD + 1, 8 * WBLK, C_IN), BF16),
+            pltpu.VMEM(((PLANES + 1) * depth, WBLK + 1, 8, C_IN), F32),
+            pltpu.VMEM((WSLOTS * PIECE, C_IN), F32),
+            pltpu.VMEM((n_tile, WSLOTS * PIECE, C_IN), BF16),
+            pltpu.VMEM((STOPS, WSLOTS * PIECE, C_IN), BF16),
+            pltpu.VMEM((STOPS * 2 * WSLOTS, 16, C_IN), F32),
+            dma((n_tile,)),
+            dma((n_tile,)),
+            dma,
+            dma((TH * FMOD,)),
+            dma((lines // RMOD + 1,)),
+            dma((TH,)),
+            dma((n_tile,)),
+            dma((STOPS,)),
+        ],
+        compiler_params=pltpu.CompilerParams(collective_id=1, has_side_effects=True, vmem_limit_bytes=VMEM_BYTES),
+        cost_estimate=pl.CostEstimate(flops=0, bytes_accessed=16 * 1024 * 1024, transcendentals=0),
+        name="exchange",
+    )(strip, mine, meta)
 
 
 def shards(
@@ -428,20 +617,24 @@
     upstream,
 ):
     peer_count = lax.axis_size("tile")
-    frames = input_video[0]
+    me = lax.axis_index("tile")
+    strip = input_video[0].reshape(PLANES, FMOD, TH, 8 * WBLK, C_IN)
     clip_ids = block_clip[0]
-    rimmed = extended(frames, (("tile", 1),), 1)
-    padded = jnp.pad(rimmed, ((2, 0), (0, 0), (1, 1), (0, 0)))
-    send_plan = send_slot[0, 0]
-    capacity = send_plan.shape[1]
-    chosen = jnp.minimum(send_plan.reshape(-1), TBLK * WBLK - 1)
-    zero_rows = jnp.zeros_like(chosen)
-    outgoing = jax.vmap(partial(cut_tile, padded, clip_ids))(zero_rows, chosen)
-    outgoing = outgoing.reshape((peer_count, capacity) + outgoing.shape[1:])
-    arrived = lax.all_to_all(outgoing, "tile", split_axis=0, concat_axis=0, tiled=True)
-    arrived = arrived.reshape((peer_count * capacity,) + arrived.shape[2:])
-    work_tiles = arrived[recv_index[0, 0]]
-
+    mine = jnp.concatenate(
+        [send_slot[0, 0].reshape(-1), recv_index[0, 0], jnp.zeros((128 - 2 * peer_count - WSLOTS,), jnp.int32)]
+    )[None]
+    depth = peer_count * TH // RMOD + 2
+    block = jnp.arange(TBLK, dtype=jnp.int32)
+    place = (me % FMOD - TT * block + 2) % FMOD
+    linked = jnp.concatenate([jnp.zeros((1,), bool), clip_ids[1:] == clip_ids[:-1]])
+    plane = jnp.where((place >= 2) | linked, (TT * block - 2 + place) // FMOD, PLANES)
+    owner = jnp.arange(peer_count, dtype=jnp.int32)
+    top = owner * TH - 1
+    line = (top + (me // FMOD - top) % RMOD - me // FMOD + RMOD) // RMOD
+    meta = jnp.concatenate(
+        [plane * depth, jnp.zeros((2,), jnp.int32), line, jnp.zeros((120 - peer_count,), jnp.int32)]
+    )[None]
+    work_tiles = exchange_call(peer_count, strip, mine, meta)
     clips = jnp.arange(CLIPS, dtype=jnp.int32)[:, None, None]
     member = jnp.broadcast_to((tile_clip[0, 0][None, :, None] == clips).astype(F32), (CLIPS, WSLOTS, C_OUT))
     affine = jnp.concatenate([norm_gain[None], norm_shift[None], jnp.zeros((6, C_OUT), F32)], axis=0)

time: 323 us -> 217 us (0.67)
  waiting for transfers between devices: 118 us -> 0 us
  Pallas kernels: 91.8 us -> 203 us
  local copies, waits for them, and re-layouts: 71.1 us -> 7.57 us
  other arithmetic: 25 us -> 4.21 us
  starting transfers between devices: 13.5 us -> 0 us
    all_to_all x1 -> x0, waiting for transfers between devices: 118 us -> none  [shards(): lax.all_to_all(outgoing, 'tile', split_axis=0, concat_axis=0, tiled=True)]
    pallas_call x0 -> x1, Pallas kernels: none -> 96.7 us  [exchange_call(): pl.pallas_call(partial(exchange_kernel, n_tile, lines), out_shape=jax.Sha...]
    gather x4 -> x0, local copies, waits for them, and re-layouts: 19.5 us -> none  [the longest x1 10.2 us: cut_tile(): lax.dynamic_slice(padded, (block_id * TT, strip_row, width_block * TW, ze...]
    reshape x1 -> x0, local copies, waits for them, and re-layouts: 18 us -> none  [shards(): outgoing = outgoing.reshape((peer_count, capacity) + outgoing.shape[1:])]
    concatenate x3 -> x0, other arithmetic: 17.4 us -> none  [the longest x1 10.2 us: extended(): jnp.concatenate([lax.ppermute(tail, axis, [(i, (i + 1) % count) for i in...]
    pallas_call x1, Pallas kernels: 91.8 us -> 106 us  [main_call(): pl.pallas_call(partial(main_kernel, n_tile, n_rep), out_shape=(jax.ShapeD...]
    all_to_all x1 -> x0, local copies, waits for them, and re-layouts: 11.3 us -> none  [shards(): lax.all_to_all(outgoing, 'tile', split_axis=0, concat_axis=0, tiled=True)]
    ppermute x2 -> x0, starting transfers between devices: 7.66 us -> none  [the longest x1 5.74 us: extended(): lax.ppermute(head, axis, [((i + 1) % count, i) for i in range(ends)])]
  transfers between devices with their start and end apart: 3 -> 0, of which waited for: 1 -> 0; matrix products, arithmetic and copies ran while one was open for 3% -> 0% of each run, Pallas kernels for 0% -> 0%
where the time goes in v2:
time: 217 us; the launch traced here: 215 us
  Pallas kernels  203 us (94%)
  local copies, waits for them, and re-layouts  7.57 us (3%)
  other arithmetic  4.21 us (2%)
    pallas_call x1, Pallas kernels, main_call(): pl.pallas_call(partial(main_kernel, n_tile, n_rep), out_shape=(jax.ShapeD...  106 us
    pallas_call x1, Pallas kernels, exchange_call(): pl.pallas_call(partial(exchange_kernel, n_tile, lines), out_shape=jax.Sha...  96.7 us

profile of v2, /device:TPU:24, one launch (start us, length us, event | category | flops | bytes accessed | tf_op | source)
XLA Modules:
  0.0 215.0 jit_solution(6706567339702048848)
XLA Ops:
  0.7 0.8 compare_bitcast_fusion
  1.5 0.1 fusion.3
  1.6 0.1 pad.2.clone
  1.7 0.7 fusion
  2.3 1.4 maximum_maximum_fusion.affine
  3.7 0.8 copy.13
  4.4 0.1 reshape_squeeze.7
  4.6 1.3 add_bitcast_fusion
  5.9 0.7 broadcast_in_dim.36.member
  6.5 96.7 %exchange.1.tiles = bf16[16,6,10,10,128]{4,3,2,1,0:T(8,128)(2,1)} custom-call(bf16[4,6,8,64,128]{4,3,2,1,0:T(8,128)(2,1)} %bitcast.15, s32[1,128]{1,0:T(1,128)} %get-tuple-element.9.mine, s32[1,128]{1,0:T(1,128)} %get-tuple-element.10.meta), custom_call_target="tpu_custom_call" | custom-call | bytes 16777216 | tf_op jit(solution)/shard_map/exchange/pallas_call | solution.py:579
  103.3 105.8 %conv_norm.1 = (bf16[16,256,256]{2,1,0:T(8,128)(2,1)}, f32[112,256]{1,0:T(8,128)}, f32[8,256]{1,0:T(8,128)}) custom-call(bf16[16,6,10,10,128]{4,3,2,1,0:T(8,128)(2,1)} %exchange.1.tiles, bf16[3456,256]{1,0:T(8,128)(2,1)} %filt.1, bf16[16,256,256]{2,1,0:T(8,128)(2,1)} %bitcast.21, f32[3,16,256]{2,1,0:T(8,128)} %broadcast_in_dim.36.member, ...), custom_call_target="tpu_custom_call" | custom-call | flops 14495514624 | bytes 16777216 | tf_op jit(solution)/shard_map/conv_norm/pallas_call | solution.py:344
  209.1 1.3 slice.13
  210.4 1.6 constant_dynamic-slice_fusion
  211.9 3.1 %copy.15 = bf16[1,1,16,256,256]{4,3,2,1,0:T(8,128)(2,1)} copy(bf16[1,1,16,256,256]{4,3,2,1,0:T(8,128)(2,1)} %bitcast.16) | data formatting | bytes 4194304
  (5 shorter events, 0.0 us)

commit v3 on v2

--- a/solution.py
+++ b/solution.py
@@ -29,6 +29,7 @@
 TAP = [(a, e, q) for a in range(3) for e in range(3) for q in range(3)]
 F32, BF16 = jnp.float32, jnp.bfloat16
 ROWS = 27 * C_IN
+SIDE = 4
 GVOX = float(VOX * CPG)
 SLAB = 60 * 8
 VMEM_BYTES = 60 * 1024 * 1024
@@ -85,8 +86,8 @@
 
 def main_kernel(
     n_tile, n_rep, tiles, filt, up, member, affine, act, grad, norm,
-    even, odd, conv, ngrad, cgrad, sums, sq, tmean, tinv, blk, buf, half, other, part, red, zin, zout, fin, nbuf, blk2, buf2,
-    g_send, g_recv, h_send, h_recv, c_send, c_recv, p_send, p_recv, z_send, z_recv, y_send, y_recv, f_send, f_recv, n_send, n_recv,
+    even, odd, conv, ngrad, cgrad, sums, sq, tmean, tinv, blk, buf, half, other, part, ring, part2, red, zin, zout, nbuf, blk2, buf2,
+    g_send, g_recv, h_send, h_recv, c_send, c_recv, p_send, p_recv, r_send, r_recv, z_send, z_recv, y_send, y_recv, n_send, n_recv,
 ):
     me = lax.axis_index("tile")
     rep = lax.axis_index("rep")
@@ -106,15 +107,34 @@
         pl.semaphore_signal(barrier, inc=1, device_id={"rep": lax.rem(rep + s, n_rep)}, device_id_type=MESH)
         return c
 
+    def greet_mate(s, c):
+        where = {"tile": mate, "rep": lax.rem(rep + s, n_rep)}
+        pl.semaphore_signal(barrier, inc=1, device_id=where, device_id_type=MESH)
+        return c
+
     lax.fori_loop(1, n_tile, greet_tile, 0)
     lax.fori_loop(1, n_rep, greet_rep, 0)
+    lax.fori_loop(1, n_rep, greet_mate, 0)
 
     gi = lax.broadcasted_iota(jnp.int32, (C_OUT, C_OUT), 0) >> 3
     gj = lax.broadcasted_iota(jnp.int32, (C_OUT, C_OUT), 1) >> 3
     same_group = (gi == gj).astype(F32)
 
+    def exact(v, w):
+        return jnp.dot(v, w, precision=lax.Precision.HIGHEST, preferred_element_type=F32)
+
     def per_group(v):
-        return jnp.dot(v, same_group, precision=lax.Precision.HIGHEST, preferred_element_type=F32)
+        return exact(v, same_group)
+
+    def packed(rows):
+        ch = lax.broadcasted_iota(jnp.int32, (C_OUT, 128), 0) >> 3
+        lane = lax.broadcasted_iota(jnp.int32, (C_OUT, 128), 1)
+        return sum(exact(rows[k], (lane == ch + k * GROUPS).astype(F32)) for k in range(CLIPS))
+
+    def unpacked(v, k):
+        lane = lax.broadcasted_iota(jnp.int32, (128, C_OUT), 0)
+        ch = lax.broadcasted_iota(jnp.int32, (128, C_OUT), 1) >> 3
+        return exact(v, (lane == ch + k * GROUPS).astype(F32))
 
     def forward(n, c):
         for j in range(4):
@@ -141,31 +161,30 @@
         return c
 
     lax.fori_loop(0, WSLOTS, centre, 0)
-    gsq = per_group(sq[...])
-    counts, firsts, seconds = [], [], []
+    local = []
     for k in range(CLIPS):
         m = member[k]
         n_k = jnp.sum(m, axis=0, keepdims=True)
-        s_k = jnp.sum(m * gsum, axis=0, keepdims=True)
-        mu = s_k / (GVOX * jnp.maximum(n_k, 1.0))
+        mu = jnp.sum(m * gsum, axis=0, keepdims=True) / (GVOX * jnp.maximum(n_k, 1.0))
         off = tmean[...] - mu
-        counts.append(n_k)
-        firsts.append(s_k)
-        seconds.append(jnp.sum(m * (gsq + GVOX * off * off), axis=0, keepdims=True))
-    blk[...] = jnp.concatenate(counts + firsts + seconds + [jnp.zeros((7, C_OUT), F32)], axis=0)
-
-    pl.semaphore_wait(barrier, n_tile + n_rep - 2)
+        first = jnp.sum(m * sums[...], axis=0, keepdims=True)
+        second = jnp.sum(m * (sq[...] + float(VOX) * off * off), axis=0, keepdims=True)
+        local.append(jnp.concatenate([n_k / float(CPG), first, second, jnp.zeros((5, C_OUT), F32)], axis=0))
+    blk[...] = packed(local)
+
+    pl.semaphore_wait(barrier, n_tile + 2 * n_rep - 3)
     gather_block(blk, buf, g_send, g_recv, me, n_tile)
 
-    all_n = buf[:, 0:3, :]
-    all_s = buf[:, 3:6, :]
-    n_tot = jnp.sum(all_n, axis=0)
+    all_n = buf[:, 0:1, :]
+    all_s = buf[:, 1:2, :]
+    n_tot = jnp.maximum(jnp.sum(all_n, axis=0), 1.0)
     mean = jnp.sum(all_s, axis=0) / (GVOX * n_tot)
     off = all_s / (GVOX * jnp.maximum(all_n, 1.0)) - mean
-    var = jnp.sum(buf[:, 6:9, :] + GVOX * all_n * off * off, axis=0) / (GVOX * n_tot)
-    inv = lax.rsqrt(var + epsilon)
-    tmean[...] = sum(member[k] * mean[k : k + 1] for k in range(CLIPS))
-    tinv[...] = sum(member[k] * inv[k : k + 1] for k in range(CLIPS))
+    var = jnp.sum(buf[:, 2:3, :] + GVOX * all_n * off * off, axis=0) / (GVOX * n_tot)
+    table = jnp.concatenate([mean, lax.rsqrt(var + epsilon), jnp.zeros((6, 128), F32)], axis=0)
+    wide_table = [unpacked(table, k) for k in range(CLIPS)]
+    tmean[...] = sum(member[k] * wide_table[k][0:1] for k in range(CLIPS))
+    tinv[...] = sum(member[k] * wide_table[k][1:2] for k in range(CLIPS))
 
     gain = affine[0:1, :]
     shift = affine[1:2, :]
@@ -192,14 +211,15 @@
     lax.fori_loop(0, WSLOTS, middle, 0)
     firsts = [jnp.sum(member[k] * sums[...], axis=0, keepdims=True) for k in range(CLIPS)]
     crosses = [jnp.sum(member[k] * sq[...], axis=0, keepdims=True) for k in range(CLIPS)]
-    blk2[...] = jnp.concatenate(firsts + crosses + [jnp.zeros((2, C_OUT), F32)], axis=0)
+    zeros = jnp.zeros((6, C_OUT), F32)
+    scaled = packed([jnp.concatenate([firsts[k] * gain, crosses[k] * gain, zeros], axis=0) for k in range(CLIPS)])
+    over_clips = [sum(crosses), sum(firsts)]
+    halves = [v[:, lo : lo + 128] for v in over_clips for lo in (0, 128)]
+    blk2[...] = jnp.concatenate([scaled[0:2]] + halves + [jnp.zeros((2, 128), F32)], axis=0)
     gather_block(blk2, buf2, h_send, h_recv, me, n_tile)
     total = jnp.sum(buf2[...], axis=0)
 
-    both = jnp.concatenate(
-        [jnp.sum(total[3:6], axis=0, keepdims=True), jnp.sum(total[0:3], axis=0, keepdims=True), jnp.zeros((6, C_OUT), F32)], axis=0
-    )
-    nbuf[rep] = both
+    nbuf[rep] = total
 
     def norm_start(s, c):
         to = lax.rem(rep + s, n_rep)
@@ -214,12 +234,10 @@
 
     lax.fori_loop(1, n_rep, norm_start, 0)
 
-    scaled = per_group(total * gain)
-    spread_n = GVOX * n_tot
-    mg = scaled[0:3] / spread_n
-    mc = scaled[3:6] / spread_n
-    sums[...] = sum(member[k] * mg[k : k + 1] for k in range(CLIPS))
-    sq[...] = sum(member[k] * mc[k : k + 1] for k in range(CLIPS))
+    table = total / (GVOX * n_tot)
+    wide_table = [unpacked(table, k) for k in range(CLIPS)]
+    sums[...] = sum(member[k] * wide_table[k][0:1] for k in range(CLIPS))
+    sq[...] = sum(member[k] * wide_table[k][1:2] for k in range(CLIPS))
 
     def conv_gradient(i, c):
         iv = tinv[pl.ds(i, 1), :]
@@ -234,62 +252,107 @@
 
     share = ROWS // chips
 
-    def mate_copy(p):
-        rows = pl.ds(p * C_IN, (min(p + 2, 27) - p) * C_IN)
-        return remote(half.at[1 - core, rows], other.at[rows], c_send.at[p // 2], c_recv.at[p // 2], tile=mate)
-
-    def chip_copy(j, k):
-        return remote(half.at[core, pl.ds(j * share, share)], part.at[k], p_send.at[j], p_recv.at[k], tile=j * 2 + core)
+    batches = [(0, 8), (8, 16), (16, 22), (22, 27)]
+
+    def mate_copy(b):
+        lo, hi = batches[b]
+        rows = pl.ds(lo * C_IN, (hi - lo) * C_IN)
+        return remote(half.at[1 - core, rows], other.at[rows], c_send.at[b], c_recv.at[b], tile=mate)
+
+    row, col = lax.div(chip, SIDE), lax.rem(chip, SIDE)
+    u = col + core * (row - col)
+    v = row + core * (col - row)
+
+    def chip_at(pu, pv):
+        return pu * (1 + (SIDE - 1) * core) + pv * (SIDE - (SIDE - 1) * core)
+
+    def place(j):
+        return j % SIDE + core * (j // SIDE - j % SIDE), j // SIDE + core * (j % SIDE - j // SIDE)
+
+    def ring_copy(j, slot, pu, pv):
+        to = chip_at(pu, v) * 2 + core
+        at = slot * SIDE + pv
+        return remote(half.at[core, pl.ds(j * share, share)], part.at[at], p_send.at[j], p_recv.at[at], tile=to)
+
+    def cross_copy(slot, pv):
+        to = chip_at(u, pv) * 2 + core
+        return remote(ring.at[pv], part2.at[slot], r_send.at[pv], r_recv.at[slot], tile=to)
 
     done = [0]
 
-    def settle(p):
-        lo, hi = p * C_IN, min(p + 2, 27) * C_IN
-        mate_copy(p).wait_recv()
+    def settle(b):
+        lo, hi = batches[b][0] * C_IN, batches[b][1] * C_IN
+        mate_copy(b).wait_recv()
         half[core, lo:hi, :] = half[core, lo:hi, :] + other[lo:hi, :]
         while (done[0] + 1) * share <= hi:
             j = done[0]
 
-            @pl.when(chip != j)
+            pu, pv = place(j)
+
+            @pl.when(pu != u)
             def _():
-                chip_copy(j, chip).start()
-
-            @pl.when(chip == j)
+                ring_copy(j, u, pu, pv).start()
+
+            @pl.when(pu == u)
             def _():
-                part[j] = half[core, j * share : (j + 1) * share, :]
+                part[u * SIDE + pv] = half[core, j * share : (j + 1) * share, :]
 
             done[0] += 1
 
-    lag = 4
-    for p in range(0, 27, 2):
-        d = None
-        for u in range(0, WSLOTS, 4):
-            rows = jnp.concatenate([pair_slab(even, odd, i, p) for i in range(u, u + 4)], axis=0)
-            g = jnp.concatenate([cgrad[i] for i in range(u, u + 4)], axis=0)
-            t = lax.dot_general(rows, g, (((0,), (0,)), ((), ())), preferred_element_type=F32)
-            d = t if d is None else d + t
-        lo, hi = p * C_IN, min(p + 2, 27) * C_IN
-        half[0, lo:hi, :] = d[:, :128]
-        half[1, lo:hi, :] = d[:, 128:]
-        mate_copy(p).start()
-        if p >= lag:
-            settle(p - lag)
-    for p in range(0, 27, 2):
-        if p + lag >= 27:
-            settle(p)
-
-    def plane_wait(s, c):
-        j = lax.rem(chip + s, chips)
-        chip_copy(j, chip).wait_send()
-        chip_copy(j, j).wait_recv()
-        return c
-
-    lax.fori_loop(1, chips, plane_wait, 0)
-    for p in range(0, 27, 2):
-        mate_copy(p).wait_send()
+    for b, (first_tap, end_tap) in enumerate(batches):
+        for p in range(first_tap, end_tap, 2):
+            d = None
+            for n in range(0, WSLOTS, 4):
+                rows = jnp.concatenate([pair_slab(even, odd, i, p) for i in range(n, n + 4)], axis=0)
+                g = jnp.concatenate([cgrad[i] for i in range(n, n + 4)], axis=0)
+                t = lax.dot_general(rows, g, (((0,), (0,)), ((), ())), preferred_element_type=F32)
+                d = t if d is None else d + t
+            lo, hi = p * C_IN, min(p + 2, 27) * C_IN
+            half[0, lo:hi, :] = d[:, :128]
+            half[1, lo:hi, :] = d[:, 128:]
+        mate_copy(b).start()
+        if b > 0:
+            settle(b - 1)
+    settle(len(batches) - 1)
+
+    def ring_sum(s, c):
+        pv = lax.rem(v + s, SIDE)
+        for t in range(1, SIDE):
+            pu = lax.rem(u + t, SIDE)
+            ring_copy(0, pu, pu, pv).wait_recv()
+        ring[pv] = sum(part[pu * SIDE + pv] for pu in range(SIDE))
+
+        @pl.when(pv != v)
+        def _():
+            cross_copy(v, pv).start()
+
+        @pl.when(pv == v)
+        def _():
+            part2[v] = ring[v]
+
+        return c
+
+    lax.fori_loop(1, SIDE + 1, ring_sum, 0)
+    for j in range(chips):
+        pu, pv = place(j)
+
+        @pl.when(pu != u)
+        def _():
+            ring_copy(j, u, pu, pv).wait_send()
+
+    for b in range(len(batches)):
+        mate_copy(b).wait_send()
+
+    def cross_wait(s, c):
+        pv = lax.rem(v + s, SIDE)
+        cross_copy(v, pv).wait_send()
+        cross_copy(pv, pv).wait_recv()
+        return c
+
+    lax.fori_loop(1, SIDE, cross_wait, 0)
 
     piece = red.shape[0] // n_rep
-    red[0:share, :] = jnp.sum(part[...], axis=0)
+    red[0:share, :] = jnp.sum(part2[...], axis=0)
     if red.shape[0] > share:
         red[share:, :] = jnp.zeros((red.shape[0] - share, 128), F32)
     zin[rep] = red[pl.ds(pl.multiple_of(rep * piece, 8), piece), :]
@@ -297,10 +360,16 @@
     def z_copy(to, slot, s):
         return remote(red.at[pl.ds(pl.multiple_of(to * piece, 8), piece)], zin.at[slot], z_send.at[s], z_recv.at[slot], rep=to)
 
-    def y_copy(to, slot, s):
-        rows = pl.ds(pl.multiple_of(slot * piece, 8), piece)
-        mine = pl.ds(pl.multiple_of(rep * piece, 8), piece)
-        return remote(zout.at[mine], zout.at[rows], y_send.at[s], y_recv.at[slot], rep=to)
+    def rows_at(r):
+        return pl.ds(pl.multiple_of(r * piece, 8), piece)
+
+    def y_copy(side, to, slot, s):
+        tile = me if side == 0 else mate
+        from_core = core if side == 0 else 1 - core
+        mine = zout.at[core, rows_at(rep)]
+        there = zout.at[core, rows_at(rep)] if slot is None else zout.at[from_core, rows_at(slot)]
+        got = core * n_rep + rep if slot is None else from_core * n_rep + slot
+        return remote(mine, there, y_send.at[side * n_rep + s], y_recv.at[got], tile=tile, rep=to)
 
     def each(what):
         def body(s, c):
@@ -314,24 +383,20 @@
     norm[...] = jnp.sum(nbuf[...], axis=0)
     each(lambda to, s: z_copy(to, rep, s).wait_send())
     each(lambda to, s: z_copy(to, to, s).wait_recv())
-    zout[pl.ds(pl.multiple_of(rep * piece, 8), piece), :] = jnp.sum(zin[...], axis=0)
-    each(lambda to, s: y_copy(to, rep, s).start())
-    each(lambda to, s: y_copy(to, rep, s).wait_send())
-    each(lambda to, s: y_copy(to, to, s).wait_recv())
+    zout[core, rows_at(rep), :] = jnp.sum(zin[...], axis=0)
+    y_copy(1, rep, None, 0).start()
+    for side in range(2):
+        each(lambda to, s: y_copy(side, to, None, s).start())
+    y_copy(1, rep, None, 0).wait_send()
+    y_copy(1, rep, rep, 0).wait_recv()
+    for side in range(2):
+        each(lambda to, s: y_copy(side, to, None, s).wait_send())
+        each(lambda to, s: y_copy(side, to, to, s).wait_recv())
 
     keep = grad.shape[0]
-    skip = share - keep
-
-    def rows_of(c):
-        return pl.ds(pl.multiple_of(c * skip, 8), keep)
-
-    swap = remote(zout.at[rows_of(1 - core)], fin, f_send, f_recv, tile=mate)
-    swap.start()
-    swap.wait()
-    own = zout[rows_of(core), :]
-    there = fin[...]
-    grad[:, 0:128] = jnp.where(core == 0, own, there)
-    grad[:, 128:256] = jnp.where(core == 0, there, own)
+    own = pl.ds(pl.multiple_of(core * (share - keep), 8), keep)
+    grad[:, 0:128] = zout[0, own, :]
+    grad[:, 128:256] = zout[1, own, :]
 
 
 def main_call(n_tile, n_rep, tiles, filt, up, member, affine):
@@ -346,7 +411,7 @@
         out_shape=(
             jax.ShapeDtypeStruct((WSLOTS, VOX, C_OUT), BF16),
             jax.ShapeDtypeStruct((keep, C_OUT), F32),
-            jax.ShapeDtypeStruct((8, C_OUT), F32),
+            jax.ShapeDtypeStruct((8, 128), F32),
         ),
         in_specs=[whole] * 5,
         out_specs=(whole,) * 3,
@@ -360,24 +425,26 @@
             pltpu.VMEM((WSLOTS, C_OUT), F32),
             pltpu.VMEM((WSLOTS, C_OUT), F32),
             pltpu.VMEM((WSLOTS, C_OUT), F32),
-            pltpu.VMEM((16, C_OUT), F32),
-            pltpu.VMEM((n_tile, 16, C_OUT), F32),
+            pltpu.VMEM((8, 128), F32),
+            pltpu.VMEM((n_tile, 8, 128), F32),
             pltpu.VMEM((2, ROWS, 128), F32),
             pltpu.VMEM((ROWS, 128), F32),
             pltpu.VMEM((chips, share, 128), F32),
+            pltpu.VMEM((SIDE, share, 128), F32),
+            pltpu.VMEM((SIDE, share, 128), F32),
             pltpu.VMEM((padded, 128), F32),
             pltpu.VMEM((n_rep, padded // n_rep, 128), F32),
-            pltpu.VMEM((padded, 128), F32),
-            pltpu.VMEM((keep, 128), F32),
-            pltpu.VMEM((n_rep, 8, C_OUT), F32),
-            pltpu.VMEM((8, C_OUT), F32),
-            pltpu.VMEM((n_tile, 8, C_OUT), F32),
+            pltpu.VMEM((2, padded, 128), F32),
+            pltpu.VMEM((n_rep, 8, 128), F32),
+            pltpu.VMEM((8, 128), F32),
+            pltpu.VMEM((n_tile, 8, 128), F32),
         ]
         + [dma((n_tile,))] * 4
         + [dma((14,))] * 2
         + [dma((chips,))] * 2
-        + [dma((n_rep,))] * 4
-        + [dma] * 2
+        + [dma((SIDE,))] * 2
+        + [dma((n_rep,))] * 2
+        + [dma((2 * n_rep,))] * 2
         + [dma((n_rep,))] * 2,
         compiler_params=pltpu.CompilerParams(collective_id=0, has_side_effects=True, vmem_limit_bytes=VMEM_BYTES),
         cost_estimate=pl.CostEstimate(flops=4 * WSLOTS * VOX * ROWS * C_OUT, bytes_accessed=16 * 1024 * 1024, transcendentals=WSLOTS * VOX * C_OUT),
@@ -390,6 +457,16 @@
 STOPS = FMOD * RMOD
 PIECE = 20
 PLANES = FRAMES // FMOD
+
+
+def ordered_peer(me, s):
+    core, chip = lax.rem(me, 2), lax.div(me, 2)
+    row, col = lax.div(chip, SIDE), lax.rem(chip, SIDE)
+    n = lax.div(s, 2)
+    p, q = lax.rem(n, SIDE), lax.rem(n + lax.div(n, SIDE), SIDE)
+    x = lax.rem(col + p + core * (q - p), SIDE)
+    y = lax.rem(row + q + core * (p - q), SIDE)
+    return (y * SIDE + x) * 2 + lax.rem(core + lax.rem(s, 2), 2)
 
 
 def exchange_kernel(
@@ -427,27 +504,31 @@
 
     lax.fori_loop(1, n_tile, table_start, 0)
 
-    def line(h):
-        y = me * TH + h
-        return lax.rem(y, RMOD) * FMOD, lax.div(y, RMOD)
-
-    def spread(n, c):
-        h = lax.div(n, FMOD)
-        a = lax.rem(n + me, FMOD)
-        stop, index = line(h)
-        to = stop + a
-
-        @pl.when(to != me)
+    def lines_to(to, what):
+        a = lax.rem(to, FMOD)
+        h0 = lax.rem(lax.div(to, FMOD) + RMOD * TH - lax.rem(me * TH, RMOD), RMOD)
+
+        @pl.when(to < STOPS)
         def _():
-            remote(strip.at[:, a, h], raw.at[:, index], v_send.at[n], v_recv.at[index], tile=to).start()
-
-        @pl.when(to == me)
-        def _():
-            pltpu.make_async_copy(strip.at[:, a, h], raw.at[:, index], v_own.at[h]).start()
-
-        return c
-
-    lax.fori_loop(0, TH * FMOD, spread, 0)
+            what(a, h0, lax.div(me * TH + h0, RMOD))
+
+            @pl.when(h0 < TH - RMOD)
+            def _():
+                what(a, h0 + RMOD, lax.div(me * TH + h0 + RMOD, RMOD))
+
+    def line_copy(to, a, h, index):
+        return remote(strip.at[:, a, h], raw.at[:, index], v_send.at[h * FMOD + a], v_recv.at[index], tile=to)
+
+    def spread(s, c):
+        to = ordered_peer(me, s)
+        lines_to(to, lambda a, h, index: line_copy(to, a, h, index).start())
+        return c
+
+    def keep(a, h, index):
+        pltpu.make_async_copy(strip.at[:, a, h], raw.at[:, index], v_own.at[h]).start()
+
+    lax.fori_loop(1, n_tile, spread, 0)
+    lines_to(me, keep)
 
     def clear(i, c):
         wide[i] = jnp.zeros(wide.shape[1:], F32)
@@ -488,7 +569,7 @@
     @pl.when(me < STOPS)
     def _():
         def serve(s, c):
-            w = lax.rem(me + s, n_tile)
+            w = ordered_peer(me, lax.rem(s, n_tile))
             for j in range(WSLOTS):
                 r = stab[w, 0, 64 + j]
                 t = lax.div(r, 2)
@@ -514,7 +595,7 @@
         lax.fori_loop(1, n_tile + 1, serve, 0)
 
     def land(s, c):
-        i = lax.rem(me + n_tile - s, n_tile)
+        i = ordered_peer(me, lax.rem(s, n_tile))
 
         @pl.when(i < STOPS)
         def _():
@@ -547,19 +628,12 @@
 
     lax.fori_loop(0, WSLOTS, build, 0)
 
-    def sent(n, c):
-        h = lax.div(n, FMOD)
-        a = lax.rem(n + me, FMOD)
-        stop, index = line(h)
-        to = stop + a
-
-        @pl.when(to != me)
-        def _():
-            remote(strip.at[:, a, h], raw.at[:, index], v_send.at[n], v_recv.at[index], tile=to).wait_send()
-
-        return c
-
-    lax.fori_loop(0, TH * FMOD, sent, 0)
+    def sent(s, c):
+        to = ordered_peer(me, s)
+        lines_to(to, lambda a, h, index: line_copy(to, a, h, index).wait_send())
+        return c
+
+    lax.fori_loop(1, n_tile, sent, 0)
 
     @pl.when(me < STOPS)
     def _():
@@ -644,7 +718,7 @@
     row_share = ROWS // peer_count
     skip = (grad_rows.shape[0] - row_share) * lax.rem(lax.axis_index("tile"), 2)
     grad_shard = lax.dynamic_slice_in_dim(grad_rows, skip, row_share, 0)
-    return (activation[None, None], grad_shard, norm_rows[:2])
+    return (activation[None, None], grad_shard, norm_rows[2:6].reshape(2, C_OUT))
 
 
 def solution(mesh):

time: 217 us -> 183 us (0.84)
  Pallas kernels: 203 us -> 170 us
    pallas_call x1, Pallas kernels: 106 us -> 75.9 us  [main_call(): pl.pallas_call(partial(main_kernel, n_tile, n_rep), out_shape=(jax.ShapeD...]
    pallas_call x1, Pallas kernels: 96.7 us -> 93.9 us  [exchange_call(): pl.pallas_call(partial(exchange_kernel, n_tile, lines), out_shape=jax.Sha...]
where the time goes in v3:
time: 183 us; the launch traced here: 182 us
  Pallas kernels  170 us (93%)
  local copies, waits for them, and re-layouts  7.57 us (4%)
  other arithmetic  4.21 us (2%)
    pallas_call x1, Pallas kernels, exchange_call(): pl.pallas_call(partial(exchange_kernel, n_tile, lines), out_shape=jax.Sha...  93.9 us
    pallas_call x1, Pallas kernels, main_call(): pl.pallas_call(partial(main_kernel, n_tile, n_rep), out_shape=(jax.ShapeD...  75.9 us
    unnamed x2, local copies, waits for them, and re-layouts  3.85 us

profile of v3, /device:TPU:24, one launch (start us, length us, event | category | flops | bytes accessed | tf_op | source)
XLA Modules:
  0.0 182.4 jit_solution(6821248710934851803)
XLA Ops:
  0.7 0.8 compare_bitcast_fusion
  1.5 0.1 fusion.3
  1.6 0.1 pad.2.clone
  1.7 0.7 fusion
  2.3 1.4 maximum_maximum_fusion.affine
  3.7 0.8 copy.13
  4.4 0.1 reshape_squeeze.7
  4.6 1.3 add_bitcast_fusion
  5.9 0.7 broadcast_in_dim.36.member
  6.5 93.9 %exchange.1.tiles = bf16[16,6,10,10,128]{4,3,2,1,0:T(8,128)(2,1)} custom-call(bf16[4,6,8,64,128]{4,3,2,1,0:T(8,128)(2,1)} %bitcast.15, s32[1,128]{1,0:T(1,128)} %get-tuple-element.9.mine, s32[1,128]{1,0:T(1,128)} %get-tuple-element.10.meta), custom_call_target="tpu_custom_call" | custom-call | bytes 16777216 | tf_op jit(solution)/shard_map/exchange/pallas_call | solution.py:653
  100.5 75.9 %conv_norm.1 = (bf16[16,256,256]{2,1,0:T(8,128)(2,1)}, f32[112,256]{1,0:T(8,128)}, f32[8,128]{1,0:T(8,128)}) custom-call(bf16[16,6,10,10,128]{4,3,2,1,0:T(8,128)(2,1)} %exchange.1.tiles, bf16[3456,256]{1,0:T(8,128)(2,1)} %filt.1, bf16[16,256,256]{2,1,0:T(8,128)(2,1)} %bitcast.21, f32[3,16,256]{2,1,0:T(8,128)} %broadcast_in_dim.36.member, ...), custom_call_target="tpu_custom_call" | custom-call | flops 14495514624 | bytes 16777216 | tf_op jit(solution)/shard_map/conv_norm/pallas_call | solution.py:409
  176.4 0.7 slice.13
  177.1 0.6 reshape.39
  177.7 1.6 constant_dynamic-slice_fusion
  179.3 3.1 %copy.15 = bf16[1,1,16,256,256]{4,3,2,1,0:T(8,128)(2,1)} copy(bf16[1,1,16,256,256]{4,3,2,1,0:T(8,128)(2,1)} %bitcast.16) | data formatting | bytes 4194304
  (5 shorter events, 0.0 us)

commit v4 on v3

--- a/solution.py
+++ b/solution.py
@@ -84,10 +84,203 @@
     return jnp.concatenate([left, tap_slab(even, odd, i, TAP[p + 1])], axis=1)
 
 
+FMOD = 6
+RMOD = 5
+STOPS = FMOD * RMOD
+PIECE = 20
+PART = WSLOTS // 2
+PLANES = FRAMES // FMOD
+
+
+def ordered_peer(me, s):
+    core, chip = lax.rem(me, 2), lax.div(me, 2)
+    row, col = lax.div(chip, SIDE), lax.rem(chip, SIDE)
+    n = lax.div(s, 2)
+    p, q = lax.rem(n, SIDE), lax.rem(n + lax.div(n, SIDE), SIDE)
+    x = lax.rem(col + p + core * (q - p), SIDE)
+    y = lax.rem(row + q + core * (p - q), SIDE)
+    return (y * SIDE + x) * 2 + lax.rem(core + lax.rem(s, 2), 2)
+
+
+def exchange(
+    n_tile, me, greeted, strip, mine, meta,
+    tab, stab, raw, wide, stage, sendb, recvb, rows32,
+    t_send, t_recv, s_sem, v_send, v_recv, v_own, w_send, w_recv,
+):
+    lines = n_tile * TH
+    my_f = lax.rem(me, FMOD)
+    my_r = lax.div(me, FMOD)
+    depth = lines // RMOD + 2
+    tab[me] = mine[...]
+    greeted()
+
+    def table(to, slot, s):
+        return remote(mine, tab.at[slot], t_send.at[s], t_recv.at[slot], tile=to)
+
+    def table_start(s, c):
+        table(lax.rem(me + s, n_tile), me, s).start()
+        return c
+
+    def table_wait(s, c):
+        to = lax.rem(me + s, n_tile)
+        table(to, me, s).wait_send()
+        table(to, to, s).wait_recv()
+        return c
+
+    lax.fori_loop(1, n_tile, table_start, 0)
+
+    def lines_to(to, what):
+        a = lax.rem(to, FMOD)
+        h0 = lax.rem(lax.div(to, FMOD) + RMOD * TH - lax.rem(me * TH, RMOD), RMOD)
+
+        @pl.when(to < STOPS)
+        def _():
+            what(a, h0, lax.div(me * TH + h0, RMOD))
+
+            @pl.when(h0 < TH - RMOD)
+            def _():
+                what(a, h0 + RMOD, lax.div(me * TH + h0 + RMOD, RMOD))
+
+    def line_copy(to, a, h, index):
+        return remote(strip.at[:, a, h], raw.at[:, index], v_send.at[h * FMOD + a], v_recv.at[index], tile=to)
+
+    def spread(s, c):
+        to = ordered_peer(me, s)
+        lines_to(to, lambda a, h, index: line_copy(to, a, h, index).start())
+        return c
+
+    def keep(a, h, index):
+        pltpu.make_async_copy(strip.at[:, a, h], raw.at[:, index], v_own.at[h]).start()
+
+    lax.fori_loop(1, n_tile, spread, 0)
+    lines_to(me, keep)
+
+    def clear(i, c):
+        wide[i] = jnp.zeros(wide.shape[1:], F32)
+        return c
+
+    lax.fori_loop(0, wide.shape[0], clear, 0)
+
+    lax.fori_loop(1, n_tile, table_wait, 0)
+    scalars = pltpu.make_async_copy(tab, stab, s_sem)
+    scalars.start()
+
+    @pl.when(me < STOPS)
+    def _():
+        def arrive(i, c):
+            y = i * RMOD + my_r
+            owner = lax.div(y, TH)
+            h = lax.rem(y, TH)
+
+            @pl.when(owner != me)
+            def _():
+                remote(strip.at[:, my_f, h], raw.at[:, i], v_send.at[0], v_recv.at[i], tile=owner).wait_recv()
+
+            @pl.when(owner == me)
+            def _():
+                pltpu.make_async_copy(strip.at[:, my_f, h], raw.at[:, i], v_own.at[h]).wait()
+
+            for k in range(PLANES):
+                line = raw[k, i].astype(F32)
+                gap = jnp.zeros((1, C_IN), F32)
+                line = jnp.concatenate([gap, line, gap, jnp.zeros((6, C_IN), F32)], axis=0)
+                wide[k * depth + i + 1] = line.reshape(WBLK + 1, 8, C_IN)
+            return c
+
+        lax.fori_loop(0, lax.div(lines - my_r + RMOD - 1, RMOD), arrive, 0)
+
+    scalars.wait()
+
+    def part_copy(w, slot, h):
+        return remote(sendb.at[w * 2 + h], recvb.at[slot * 2 + h], w_send.at[w * 2 + h], w_recv.at[slot * 2 + h], tile=w)
+
+    @pl.when(me < STOPS)
+    def _():
+        def serve(step, c):
+            h = lax.div(step, n_tile)
+            w = ordered_peer(me, lax.rem(step + 1, n_tile))
+            for j in range(PART):
+                r = stab[w, 0, 64 + h * PART + j]
+                t = lax.div(r, 2)
+                slot = stab[t, 0, w * 2 + lax.rem(r, 2)]
+                base = meta[0, lax.div(slot, WBLK)] + meta[0, 8 + t]
+                first = lax.rem(slot, WBLK)
+                for half in range(2):
+                    at = j * PIECE + half * 10
+                    stage[at : at + 8, :] = wide[base + half, first]
+                    stage[at + 8 : at + 10, :] = wide[base + half, first + 1][:2]
+            sendb[w * 2 + h] = stage[...].astype(BF16)
+
+            @pl.when(w != me)
+            def _():
+                part_copy(w, me, h).start()
+
+            @pl.when(w == me)
+            def _():
+                recvb[me * 2 + h] = sendb[me * 2 + h]
+
+            return c
+
+        lax.fori_loop(0, 2 * n_tile, serve, 0)
+
+    def land(h):
+        def body(s, c):
+            i = ordered_peer(me, lax.rem(s, n_tile))
+
+            @pl.when(i < STOPS)
+            def _():
+                @pl.when(i != me)
+                def _():
+                    part_copy(i, i, h).wait_recv()
+
+                v = recvb[i * 2 + h].astype(F32)
+                for j in range(PART):
+                    for half in range(2):
+                        at = j * PIECE + half * 10
+                        rows32[i * 2 * PART + j * 2 + half, 0:10, :] = v[at : at + 10]
+
+            return c
+
+        lax.fori_loop(1, n_tile + 1, body, 0)
+
+    def tile_rows(h, j):
+        r = stab[me, 0, 64 + h * PART + j]
+        t = lax.div(r, 2)
+        b = lax.div(stab[t, 0, me * 2 + lax.rem(r, 2)], WBLK)
+        out = []
+        for f in range(TT + 2):
+            a = lax.rem(b * TT + TT + f, FMOD)
+            for y in range(TH + 2):
+                q = lax.rem(t * TH + 4 + y % RMOD, RMOD)
+                at = (q * FMOD + a) * (2 * PART) + j * 2 + y // RMOD
+                out.append(rows32[at, 0:10, :])
+        return jnp.stack(out, axis=0).reshape(TT + 2, TH + 2, TW + 2, C_IN)
+
+    def drain():
+        def sent(s, c):
+            to = ordered_peer(me, s)
+            lines_to(to, lambda a, h, index: line_copy(to, a, h, index).wait_send())
+            return c
+
+        lax.fori_loop(1, n_tile, sent, 0)
+
+        @pl.when(me < STOPS)
+        def _():
+            def served(s, c):
+                w = lax.rem(me + s, n_tile)
+                for h in range(2):
+                    part_copy(w, me, h).wait_send()
+                return c
+
+            lax.fori_loop(1, n_tile, served, 0)
+
+    return land, tile_rows, drain
+
+
 def main_kernel(
-    n_tile, n_rep, tiles, filt, up, member, affine, act, grad, norm,
+    n_tile, n_rep, strip, mine, meta, filt, up, member, affine, act, grad, norm,
     even, odd, conv, ngrad, cgrad, sums, sq, tmean, tinv, blk, buf, half, other, part, ring, part2, red, zin, zout, nbuf, blk2, buf2,
-    g_send, g_recv, h_send, h_recv, c_send, c_recv, p_send, p_recv, r_send, r_recv, z_send, z_recv, y_send, y_recv, n_send, n_recv,
+    g_send, g_recv, h_send, h_recv, c_send, c_recv, p_send, p_recv, r_send, r_recv, z_send, z_recv, y_send, y_recv, n_send, n_recv, *moving,
 ):
     me = lax.axis_index("tile")
     rep = lax.axis_index("rep")
@@ -136,9 +329,12 @@
         ch = lax.broadcasted_iota(jnp.int32, (128, C_OUT), 1) >> 3
         return exact(v, (lane == ch + k * GROUPS).astype(F32))
 
+    def greeted():
+        pl.semaphore_wait(barrier, n_tile + 2 * n_rep - 3)
+
+    land, tile_rows, drain = exchange(n_tile, me, greeted, strip, mine, meta, *moving)
+
     def forward(n, c):
-        for j in range(4):
-            shifted(n * 4 + j, tiles[n * 4 + j].astype(F32), even, odd)
         acc = None
         for p in range(0, 27, 2):
             rows = jnp.concatenate([pair_slab(even, odd, n * 4 + j, p) for j in range(4)], axis=0)
@@ -150,7 +346,16 @@
             sums[pl.ds(n * 4 + j, 1), :] = jnp.sum(one, axis=0, keepdims=True)
         return c
 
-    lax.fori_loop(0, WSLOTS // 4, forward, 0)
+    for h in range(2):
+        land(h)
+
+        def unpack(j, c):
+            shifted(h * PART + j, tile_rows(h, j), even, odd)
+            return c
+
+        lax.fori_loop(0, PART, unpack, 0)
+        lax.fori_loop(h * PART // 4, (h + 1) * PART // 4, forward, 0)
+    drain()
 
     gsum = per_group(sums[...])
     tmean[...] = gsum / GVOX
@@ -172,7 +377,6 @@
         local.append(jnp.concatenate([n_k / float(CPG), first, second, jnp.zeros((5, C_OUT), F32)], axis=0))
     blk[...] = packed(local)
 
-    pl.semaphore_wait(barrier, n_tile + 2 * n_rep - 3)
     gather_block(blk, buf, g_send, g_recv, me, n_tile)
 
     all_n = buf[:, 0:1, :]
@@ -399,7 +603,9 @@
     grad[:, 128:256] = zout[1, own, :]
 
 
-def main_call(n_tile, n_rep, tiles, filt, up, member, affine):
+def main_call(n_tile, n_rep, strip, mine, meta, filt, up, member, affine):
+    lines = n_tile * TH
+    depth = lines // RMOD + 2
     chips = n_tile // 2
     share = ROWS // chips
     keep = share // 2 + 4 if (share // 2) % 8 else share // 2
@@ -413,7 +619,7 @@
             jax.ShapeDtypeStruct((keep, C_OUT), F32),
             jax.ShapeDtypeStruct((8, 128), F32),
         ),
-        in_specs=[whole] * 5,
+        in_specs=[pl.BlockSpec(memory_space=pl.ANY), whole, pl.BlockSpec(memory_space=pltpu.SMEM)] + [whole] * 4,
         out_specs=(whole,) * 3,
         scratch_shapes=[
             pltpu.VMEM((3, WSLOTS, 480, C_IN), BF16),
@@ -445,238 +651,29 @@
         + [dma((SIDE,))] * 2
         + [dma((n_rep,))] * 2
         + [dma((2 * n_rep,))] * 2
-        + [dma((n_rep,))] * 2,
-        compiler_params=pltpu.CompilerParams(collective_id=0, has_side_effects=True, vmem_limit_bytes=VMEM_BYTES),
-        cost_estimate=pl.CostEstimate(flops=4 * WSLOTS * VOX * ROWS * C_OUT, bytes_accessed=16 * 1024 * 1024, transcendentals=WSLOTS * VOX * C_OUT),
-        name="conv_norm",
-    )(tiles, filt, up, member, affine)
-
-
-FMOD = 6
-RMOD = 5
-STOPS = FMOD * RMOD
-PIECE = 20
-PLANES = FRAMES // FMOD
-
-
-def ordered_peer(me, s):
-    core, chip = lax.rem(me, 2), lax.div(me, 2)
-    row, col = lax.div(chip, SIDE), lax.rem(chip, SIDE)
-    n = lax.div(s, 2)
-    p, q = lax.rem(n, SIDE), lax.rem(n + lax.div(n, SIDE), SIDE)
-    x = lax.rem(col + p + core * (q - p), SIDE)
-    y = lax.rem(row + q + core * (p - q), SIDE)
-    return (y * SIDE + x) * 2 + lax.rem(core + lax.rem(s, 2), 2)
-
-
-def exchange_kernel(
-    n_tile, lines, strip, mine, meta, tiles,
-    tab, stab, raw, wide, stage, sendb, recvb, rows32,
-    t_send, t_recv, s_sem, v_send, v_recv, v_own, w_send, w_recv,
-):
-    me = lax.axis_index("tile")
-    my_f = lax.rem(me, FMOD)
-    my_r = lax.div(me, FMOD)
-    depth = lines // RMOD + 2
-
-    barrier = pltpu.get_barrier_semaphore()
-
-    def greet(s, c):
-        pl.semaphore_signal(barrier, inc=1, device_id={"tile": lax.rem(me + s, n_tile)}, device_id_type=MESH)
-        return c
-
-    lax.fori_loop(1, n_tile, greet, 0)
-    tab[me] = mine[...]
-    pl.semaphore_wait(barrier, n_tile - 1)
-
-    def table(to, slot, s):
-        return remote(mine, tab.at[slot], t_send.at[s], t_recv.at[slot], tile=to)
-
-    def table_start(s, c):
-        table(lax.rem(me + s, n_tile), me, s).start()
-        return c
-
-    def table_wait(s, c):
-        to = lax.rem(me + s, n_tile)
-        table(to, me, s).wait_send()
-        table(to, to, s).wait_recv()
-        return c
-
-    lax.fori_loop(1, n_tile, table_start, 0)
-
-    def lines_to(to, what):
-        a = lax.rem(to, FMOD)
-        h0 = lax.rem(lax.div(to, FMOD) + RMOD * TH - lax.rem(me * TH, RMOD), RMOD)
-
-        @pl.when(to < STOPS)
-        def _():
-            what(a, h0, lax.div(me * TH + h0, RMOD))
-
-            @pl.when(h0 < TH - RMOD)
-            def _():
-                what(a, h0 + RMOD, lax.div(me * TH + h0 + RMOD, RMOD))
-
-    def line_copy(to, a, h, index):
-        return remote(strip.at[:, a, h], raw.at[:, index], v_send.at[h * FMOD + a], v_recv.at[index], tile=to)
-
-    def spread(s, c):
-        to = ordered_peer(me, s)
-        lines_to(to, lambda a, h, index: line_copy(to, a, h, index).start())
-        return c
-
-    def keep(a, h, index):
-        pltpu.make_async_copy(strip.at[:, a, h], raw.at[:, index], v_own.at[h]).start()
-
-    lax.fori_loop(1, n_tile, spread, 0)
-    lines_to(me, keep)
-
-    def clear(i, c):
-        wide[i] = jnp.zeros(wide.shape[1:], F32)
-        return c
-
-    lax.fori_loop(0, wide.shape[0], clear, 0)
-
-    lax.fori_loop(1, n_tile, table_wait, 0)
-    scalars = pltpu.make_async_copy(tab, stab, s_sem)
-    scalars.start()
-
-    @pl.when(me < STOPS)
-    def _():
-        def arrive(i, c):
-            y = i * RMOD + my_r
-            owner = lax.div(y, TH)
-            h = lax.rem(y, TH)
-
-            @pl.when(owner != me)
-            def _():
-                remote(strip.at[:, my_f, h], raw.at[:, i], v_send.at[0], v_recv.at[i], tile=owner).wait_recv()
-
-            @pl.when(owner == me)
-            def _():
-                pltpu.make_async_copy(strip.at[:, my_f, h], raw.at[:, i], v_own.at[h]).wait()
-
-            for k in range(PLANES):
-                line = raw[k, i].astype(F32)
-                gap = jnp.zeros((1, C_IN), F32)
-                line = jnp.concatenate([gap, line, gap, jnp.zeros((6, C_IN), F32)], axis=0)
-                wide[k * depth + i + 1] = line.reshape(WBLK + 1, 8, C_IN)
-            return c
-
-        lax.fori_loop(0, lax.div(lines - my_r + RMOD - 1, RMOD), arrive, 0)
-
-    scalars.wait()
-
-    @pl.when(me < STOPS)
-    def _():
-        def serve(s, c):
-            w = ordered_peer(me, lax.rem(s, n_tile))
-            for j in range(WSLOTS):
-                r = stab[w, 0, 64 + j]
-                t = lax.div(r, 2)
-                slot = stab[t, 0, w * 2 + lax.rem(r, 2)]
-                base = meta[0, lax.div(slot, WBLK)] + meta[0, 8 + t]
-                first = lax.rem(slot, WBLK)
-                for half in range(2):
-                    at = j * PIECE + half * 10
-                    stage[at : at + 8, :] = wide[base + half, first]
-                    stage[at + 8 : at + 10, :] = wide[base + half, first + 1][:2]
-            sendb[w] = stage[...].astype(BF16)
-
-            @pl.when(w != me)
-            def _():
-                remote(sendb.at[w], recvb.at[me], w_send.at[w], w_recv.at[me], tile=w).start()
-
-            @pl.when(w == me)
-            def _():
-                recvb[me] = sendb[me]
-
-            return c
-
-        lax.fori_loop(1, n_tile + 1, serve, 0)
-
-    def land(s, c):
-        i = ordered_peer(me, lax.rem(s, n_tile))
-
-        @pl.when(i < STOPS)
-        def _():
-            @pl.when(i != me)
-            def _():
-                remote(sendb.at[0], recvb.at[i], w_send.at[0], w_recv.at[i], tile=i).wait_recv()
-
-            v = recvb[i].astype(F32)
-            for j in range(WSLOTS):
-                for half in range(2):
-                    at = j * PIECE + half * 10
-                    rows32[i * 2 * WSLOTS + j * 2 + half, 0:10, :] = v[at : at + 10]
-
-        return c
-
-    lax.fori_loop(1, n_tile + 1, land, 0)
-
-    def build(j, c):
-        r = stab[me, 0, 64 + j]
-        t = lax.div(r, 2)
-        b = lax.div(stab[t, 0, me * 2 + lax.rem(r, 2)], WBLK)
-        for f in range(TT + 2):
-            a = lax.rem(b * TT + TT + f, FMOD)
-            for y in range(RMOD):
-                q = lax.rem(t * TH + 4 + y, RMOD)
-                at = (q * FMOD + a) * (2 * WSLOTS) + j * 2
-                for half in range(2):
-                    tiles[j, f, y + half * RMOD] = rows32[at + half, 0:10, :].astype(BF16)
-        return c
-
-    lax.fori_loop(0, WSLOTS, build, 0)
-
-    def sent(s, c):
-        to = ordered_peer(me, s)
-        lines_to(to, lambda a, h, index: line_copy(to, a, h, index).wait_send())
-        return c
-
-    lax.fori_loop(1, n_tile, sent, 0)
-
-    @pl.when(me < STOPS)
-    def _():
-        def served(s, c):
-            w = lax.rem(me + s, n_tile)
-            remote(sendb.at[w], recvb.at[me], w_send.at[w], w_recv.at[me], tile=w).wait_send()
-            return c
-
-        lax.fori_loop(1, n_tile, served, 0)
-
-
-def exchange_call(n_tile, strip, mine, meta):
-    lines = n_tile * TH
-    depth = lines // RMOD + 2
-    whole = pl.BlockSpec(memory_space=pltpu.VMEM)
-    dma = pltpu.SemaphoreType.DMA
-    return pl.pallas_call(
-        partial(exchange_kernel, n_tile, lines),
-        out_shape=jax.ShapeDtypeStruct((WSLOTS, TT + 2, TH + 2, TW + 2, C_IN), BF16),
-        in_specs=[pl.BlockSpec(memory_space=pl.ANY), whole, pl.BlockSpec(memory_space=pltpu.SMEM)],
-        out_specs=whole,
-        scratch_shapes=[
+        + [dma((n_rep,))] * 2
+        + [
             pltpu.VMEM((n_tile, 1, 128), jnp.int32),
             pltpu.SMEM((n_tile, 1, 128), jnp.int32),
             pltpu.VMEM((PLANES, lines // RMOD + 1, 8 * WBLK, C_IN), BF16),
             pltpu.VMEM(((PLANES + 1) * depth, WBLK + 1, 8, C_IN), F32),
-            pltpu.VMEM((WSLOTS * PIECE, C_IN), F32),
-            pltpu.VMEM((n_tile, WSLOTS * PIECE, C_IN), BF16),
-            pltpu.VMEM((STOPS, WSLOTS * PIECE, C_IN), BF16),
-            pltpu.VMEM((STOPS * 2 * WSLOTS, 16, C_IN), F32),
+            pltpu.VMEM((PART * PIECE, C_IN), F32),
+            pltpu.VMEM((n_tile * 2, PART * PIECE, C_IN), BF16),
+            pltpu.VMEM((STOPS * 2, PART * PIECE, C_IN), BF16),
+            pltpu.VMEM((STOPS * 2 * PART, 16, C_IN), F32),
             dma((n_tile,)),
             dma((n_tile,)),
             dma,
             dma((TH * FMOD,)),
             dma((lines // RMOD + 1,)),
             dma((TH,)),
-            dma((n_tile,)),
-            dma((STOPS,)),
+            dma((n_tile * 2,)),
+            dma((STOPS * 2,)),
         ],
-        compiler_params=pltpu.CompilerParams(collective_id=1, has_side_effects=True, vmem_limit_bytes=VMEM_BYTES),
-        cost_estimate=pl.CostEstimate(flops=0, bytes_accessed=16 * 1024 * 1024, transcendentals=0),
-        name="exchange",
-    )(strip, mine, meta)
+        compiler_params=pltpu.CompilerParams(collective_id=0, has_side_effects=True, vmem_limit_bytes=VMEM_BYTES),
+        cost_estimate=pl.CostEstimate(flops=4 * WSLOTS * VOX * ROWS * C_OUT, bytes_accessed=16 * 1024 * 1024, transcendentals=WSLOTS * VOX * C_OUT),
+        name="conv_norm",
+    )(strip, mine, meta, filt, up, member, affine)
 
 
 def shards(
@@ -708,12 +705,11 @@
     meta = jnp.concatenate(
         [plane * depth, jnp.zeros((2,), jnp.int32), line, jnp.zeros((120 - peer_count,), jnp.int32)]
     )[None]
-    work_tiles = exchange_call(peer_count, strip, mine, meta)
     clips = jnp.arange(CLIPS, dtype=jnp.int32)[:, None, None]
     member = jnp.broadcast_to((tile_clip[0, 0][None, :, None] == clips).astype(F32), (CLIPS, WSLOTS, C_OUT))
     affine = jnp.concatenate([norm_gain[None], norm_shift[None], jnp.zeros((6, C_OUT), F32)], axis=0)
     activation, grad_rows, norm_rows = main_call(
-        peer_count, lax.axis_size("rep"), work_tiles, kernel, upstream[0, 0], member, affine
+        peer_count, lax.axis_size("rep"), strip, mine, meta, kernel, upstream[0, 0], member, affine
     )
     row_share = ROWS // peer_count
     skip = (grad_rows.shape[0] - row_share) * lax.rem(lax.axis_index("tile"), 2)

time: 183 us -> 173 us (0.945)
  Pallas kernels: 170 us -> 160 us
    pallas_call x1 -> x0, Pallas kernels: 93.9 us -> none  [exchange_call(): pl.pallas_call(partial(exchange_kernel, n_tile, lines), out_shape=jax.Sha...]
    pallas_call x1, Pallas kernels: 75.9 us -> 160 us  [main_call(): pl.pallas_call(partial(main_kernel, n_tile, n_rep), out_shape=(jax.ShapeD...]
where the time goes in v4:
time: 173 us; the launch traced here: 172 us
  Pallas kernels  160 us (92%)
  local copies, waits for them, and re-layouts  7.57 us (4%)
  other arithmetic  4.24 us (2%)
    pallas_call x1, Pallas kernels, main_call(): pl.pallas_call(partial(main_kernel, n_tile, n_rep), out_shape=(jax.ShapeD...  160 us
    unnamed x2, local copies, waits for them, and re-layouts  3.85 us

profile of v4, /device:TPU:24, one launch (start us, length us, event | category | flops | bytes accessed | tf_op | source)
XLA Modules:
  0.0 172.4 jit_solution(14474613816515993931)
XLA Ops:
  0.7 0.8 compare_bitcast_fusion
  1.5 0.1 fusion.3
  1.6 0.1 pad.2.clone
  1.7 0.7 fusion
  2.3 1.4 maximum_maximum_fusion.affine
  3.7 0.8 copy.13
  4.4 0.1 reshape_squeeze.7
  4.6 1.3 add_bitcast_fusion
  5.9 0.7 broadcast_in_dim.36.member
  6.6 159.9 %conv_norm.1 = (bf16[16,256,256]{2,1,0:T(8,128)(2,1)}, f32[112,256]{1,0:T(8,128)}, f32[8,128]{1,0:T(8,128)}) custom-call(bf16[4,6,8,64,128]{4,3,2,1,0:T(8,128)(2,1)} %bitcast.20, s32[1,128]{1,0:T(1,128)} %get-tuple-element.9.mine, s32[1,128]{1,0:T(1,128)} %get-tuple-element.10.meta, bf16[3456,256]{1,0:T(8,128)(2,1)} %filt.1, bf16[16,256,256]{2,1,0:T(8,128)(2,1)} %bitcast.21, ...), custom_call_target="tpu_custom_call" | custom-call | flops 14495514624 | bytes 16777216 | tf_op jit(solution)/shard_map/conv_norm/pallas_call | solution.py:615
  166.4 0.7 slice.13
  167.1 0.6 reshape.39
  167.7 1.6 constant_dynamic-slice_fusion
  169.3 3.1 %copy.15 = bf16[1,1,16,256,256]{4,3,2,1,0:T(8,128)(2,1)} copy(bf16[1,1,16,256,256]{4,3,2,1,0:T(8,128)(2,1)} %bitcast.15) | data formatting | bytes 4194304
  (5 shorter events, 0.0 us)

commit v5 on v4

--- a/solution.py
+++ b/solution.py
@@ -88,7 +88,8 @@
 RMOD = 5
 STOPS = FMOD * RMOD
 PIECE = 20
-PART = WSLOTS // 2
+PARTS = 2
+PART = WSLOTS // PARTS
 PLANES = FRAMES // FMOD
 
 
@@ -192,7 +193,7 @@
     scalars.wait()
 
     def part_copy(w, slot, h):
-        return remote(sendb.at[w * 2 + h], recvb.at[slot * 2 + h], w_send.at[w * 2 + h], w_recv.at[slot * 2 + h], tile=w)
+        return remote(sendb.at[w * PARTS + h], recvb.at[slot * PARTS + h], w_send.at[w * PARTS + h], w_recv.at[slot * PARTS + h], tile=w)
 
     @pl.when(me < STOPS)
     def _():
@@ -209,7 +210,7 @@
                     at = j * PIECE + half * 10
                     stage[at : at + 8, :] = wide[base + half, first]
                     stage[at + 8 : at + 10, :] = wide[base + half, first + 1][:2]
-            sendb[w * 2 + h] = stage[...].astype(BF16)
+            sendb[w * PARTS + h] = stage[...].astype(BF16)
 
             @pl.when(w != me)
             def _():
@@ -217,11 +218,11 @@
 
             @pl.when(w == me)
             def _():
-                recvb[me * 2 + h] = sendb[me * 2 + h]
+                recvb[me * PARTS + h] = sendb[me * PARTS + h]
 
             return c
 
-        lax.fori_loop(0, 2 * n_tile, serve, 0)
+        lax.fori_loop(0, PARTS * n_tile, serve, 0)
 
     def land(h):
         def body(s, c):
@@ -233,7 +234,7 @@
                 def _():
                     part_copy(i, i, h).wait_recv()
 
-                v = recvb[i * 2 + h].astype(F32)
+                v = recvb[i * PARTS + h].astype(F32)
                 for j in range(PART):
                     for half in range(2):
                         at = j * PIECE + half * 10
@@ -268,7 +269,7 @@
         def _():
             def served(s, c):
                 w = lax.rem(me + s, n_tile)
-                for h in range(2):
+                for h in range(PARTS):
                     part_copy(w, me, h).wait_send()
                 return c
 
@@ -278,8 +279,8 @@
 
 
 def main_kernel(
-    n_tile, n_rep, strip, mine, meta, filt, up, member, affine, act, grad, norm,
-    even, odd, conv, ngrad, cgrad, sums, sq, tmean, tinv, blk, buf, half, other, part, ring, part2, red, zin, zout, nbuf, blk2, buf2,
+    n_tile, n_rep, strip, mine, meta, filt_hbm, up_hbm, clips, gains, shifts, act, grad, norm,
+    filt, up, member, load_sem, even, odd, conv, ngrad, cgrad, sums, sq, tmean, tinv, blk, buf, half, other, part, ring, part2, red, zin, zout, nbuf, blk2, buf2,
     g_send, g_recv, h_send, h_recv, c_send, c_recv, p_send, p_recv, r_send, r_recv, z_send, z_recv, y_send, y_recv, n_send, n_recv, *moving,
 ):
     me = lax.axis_index("tile")
@@ -331,6 +332,13 @@
 
     def greeted():
         pl.semaphore_wait(barrier, n_tile + 2 * n_rep - 3)
+
+    load_filt = pltpu.make_async_copy(filt_hbm, filt, load_sem.at[0])
+    load_up = pltpu.make_async_copy(up_hbm, up, load_sem.at[1])
+    load_filt.start()
+    load_up.start()
+    for k in range(CLIPS):
+        member[k] = jnp.broadcast_to((clips[...] == k).astype(F32), (WSLOTS, C_OUT))
 
     land, tile_rows, drain = exchange(n_tile, me, greeted, strip, mine, meta, *moving)
 
@@ -346,7 +354,9 @@
             sums[pl.ds(n * 4 + j, 1), :] = jnp.sum(one, axis=0, keepdims=True)
         return c
 
-    for h in range(2):
+    load_filt.wait()
+    load_up.wait()
+    for h in range(PARTS):
         land(h)
 
         def unpack(j, c):
@@ -390,8 +400,8 @@
     tmean[...] = sum(member[k] * wide_table[k][0:1] for k in range(CLIPS))
     tinv[...] = sum(member[k] * wide_table[k][1:2] for k in range(CLIPS))
 
-    gain = affine[0:1, :]
-    shift = affine[1:2, :]
+    gain = gains[...]
+    shift = shifts[...]
 
     def middle(i, c):
         mu = tmean[pl.ds(i, 1), :]
@@ -603,7 +613,7 @@
     grad[:, 128:256] = zout[1, own, :]
 
 
-def main_call(n_tile, n_rep, strip, mine, meta, filt, up, member, affine):
+def main_call(n_tile, n_rep, strip, mine, meta, filt, up, clips, gains, shifts):
     lines = n_tile * TH
     depth = lines // RMOD + 2
     chips = n_tile // 2
@@ -611,6 +621,7 @@
     keep = share // 2 + 4 if (share // 2) % 8 else share // 2
     padded = -(-share // (8 * n_rep)) * 8 * n_rep
     whole = pl.BlockSpec(memory_space=pltpu.VMEM)
+    hbm = pl.BlockSpec(memory_space=pl.ANY)
     dma = pltpu.SemaphoreType.DMA
     return pl.pallas_call(
         partial(main_kernel, n_tile, n_rep),
@@ -619,9 +630,13 @@
             jax.ShapeDtypeStruct((keep, C_OUT), F32),
             jax.ShapeDtypeStruct((8, 128), F32),
         ),
-        in_specs=[pl.BlockSpec(memory_space=pl.ANY), whole, pl.BlockSpec(memory_space=pltpu.SMEM)] + [whole] * 4,
+        in_specs=[hbm, whole, pl.BlockSpec(memory_space=pltpu.SMEM), hbm, hbm, whole, whole, whole],
         out_specs=(whole,) * 3,
         scratch_shapes=[
+            pltpu.VMEM((ROWS, C_OUT), BF16),
+            pltpu.VMEM((WSLOTS, VOX, C_OUT), BF16),
+            pltpu.VMEM((CLIPS, WSLOTS, C_OUT), F32),
+            dma((2,)),
             pltpu.VMEM((3, WSLOTS, 480, C_IN), BF16),
             pltpu.VMEM((3, WSLOTS, 384, C_IN), BF16),
             pltpu.VMEM((WSLOTS, VOX, C_OUT), F32),
@@ -658,8 +673,8 @@
             pltpu.VMEM((PLANES, lines // RMOD + 1, 8 * WBLK, C_IN), BF16),
             pltpu.VMEM(((PLANES + 1) * depth, WBLK + 1, 8, C_IN), F32),
             pltpu.VMEM((PART * PIECE, C_IN), F32),
-            pltpu.VMEM((n_tile * 2, PART * PIECE, C_IN), BF16),
-            pltpu.VMEM((STOPS * 2, PART * PIECE, C_IN), BF16),
+            pltpu.VMEM((n_tile * PARTS, PART * PIECE, C_IN), BF16),
+            pltpu.VMEM((STOPS * PARTS, PART * PIECE, C_IN), BF16),
             pltpu.VMEM((STOPS * 2 * PART, 16, C_IN), F32),
             dma((n_tile,)),
             dma((n_tile,)),
@@ -667,13 +682,13 @@
             dma((TH * FMOD,)),
             dma((lines // RMOD + 1,)),
             dma((TH,)),
-            dma((n_tile * 2,)),
-            dma((STOPS * 2,)),
+            dma((n_tile * PARTS,)),
+            dma((STOPS * PARTS,)),
         ],
         compiler_params=pltpu.CompilerParams(collective_id=0, has_side_effects=True, vmem_limit_bytes=VMEM_BYTES),
         cost_estimate=pl.CostEstimate(flops=4 * WSLOTS * VOX * ROWS * C_OUT, bytes_accessed=16 * 1024 * 1024, transcendentals=WSLOTS * VOX * C_OUT),
         name="conv_norm",
-    )(strip, mine, meta, filt, up, member, affine)
+    )(strip, mine, meta, filt, up, clips, gains, shifts)
 
 
 def shards(
@@ -705,11 +720,9 @@
     meta = jnp.concatenate(
         [plane * depth, jnp.zeros((2,), jnp.int32), line, jnp.zeros((120 - peer_count,), jnp.int32)]
     )[None]
-    clips = jnp.arange(CLIPS, dtype=jnp.int32)[:, None, None]
-    member = jnp.broadcast_to((tile_clip[0, 0][None, :, None] == clips).astype(F32), (CLIPS, WSLOTS, C_OUT))
-    affine = jnp.concatenate([norm_gain[None], norm_shift[None], jnp.zeros((6, C_OUT), F32)], axis=0)
     activation, grad_rows, norm_rows = main_call(
-        peer_count, lax.axis_size("rep"), strip, mine, meta, kernel, upstream[0, 0], member, affine
+        peer_count, lax.axis_size("rep"), strip, mine, meta, kernel, upstream[0, 0],
+        tile_clip[0, 0][:, None], norm_gain[None], norm_shift[None]
     )
     row_share = ROWS // peer_count
     skip = (grad_rows.shape[0] - row_share) * lax.rem(lax.axis_index("tile"), 2)

time: 173 us -> 170 us (0.983)
  other arithmetic: 4.24 us -> 2.17 us
where the time goes in v5:
time: 170 us
  Pallas kernels  159 us (94%)
  local copies, waits for them, and re-layouts  8.13 us (5%)
  other arithmetic  2.17 us (1%)
    pallas_call x1, Pallas kernels, main_call(): pl.pallas_call(partial(main_kernel, n_tile, n_rep), out_shape=(jax.ShapeD...  159 us
    unnamed x2, local copies, waits for them, and re-layouts  3.85 us

profile of v5, /device:TPU:24, one launch (start us, length us, event | category | flops | bytes accessed | tf_op | source)
XLA Modules:
  0.0 169.5 jit_solution(4172735090737827740)
XLA Ops:
  0.7 0.8 compare_bitcast_fusion
  1.5 0.1 fusion.2
  1.6 1.3 copy.15.clips
  2.9 0.8 copy.14
  3.7 0.1 reshape_squeeze.7
  3.8 1.3 add_bitcast_fusion
  5.1 158.5 %conv_norm.1 = (bf16[16,256,256]{2,1,0:T(8,128)(2,1)}, f32[112,256]{1,0:T(8,128)}, f32[8,128]{1,0:T(8,128)}) custom-call(bf16[4,6,8,64,128]{4,3,2,1,0:T(8,128)(2,1)} %bitcast.18, s32[1,128]{1,0:T(1,128)} %get-tuple-element.9.mine, s32[1,128]{1,0:T(1,128)} %get-tuple-element.10.meta, bf16[3456,256]{1,0:T(8,128)(2,1)} %filt_hbm.1, ...), custom_call_target="tpu_custom_call" | custom-call | flops 14495514624 | bytes 16777216 | tf_op jit(solution)/shard_map/conv_norm/pallas_call | solution.py:626
  163.6 0.7 slice.13
  164.3 0.6 reshape.12
  164.9 1.6 constant_dynamic-slice_fusion
  166.4 3.1 %copy.17 = bf16[1,1,16,256,256]{4,3,2,1,0:T(8,128)(2,1)} copy(bf16[1,1,16,256,256]{4,3,2,1,0:T(8,128)(2,1)} %bitcast.15) | data formatting | bytes 4194304
  (4 shorter events, 0.0 us)

commit v6 on v5

--- a/solution.py
+++ b/solution.py
@@ -365,7 +365,6 @@
 
         lax.fori_loop(0, PART, unpack, 0)
         lax.fori_loop(h * PART // 4, (h + 1) * PART // 4, forward, 0)
-    drain()
 
     gsum = per_group(sums[...])
     tmean[...] = gsum / GVOX
@@ -546,6 +545,7 @@
 
         return c
 
+    drain()
     lax.fori_loop(1, SIDE + 1, ring_sum, 0)
     for j in range(chips):
         pu, pv = place(j)

time: 170 us -> 168 us (0.988)
  Pallas kernels: 159 us -> 157 us
    pallas_call x1, Pallas kernels: 159 us -> 157 us  [main_call(): pl.pallas_call(partial(main_kernel, n_tile, n_rep), out_shape=(jax.ShapeD...]
where the time goes in v6:
time: 168 us
  Pallas kernels  157 us (93%)
  local copies, waits for them, and re-layouts  8.13 us (5%)
  other arithmetic  2.17 us (1%)
    pallas_call x1, Pallas kernels, main_call(): pl.pallas_call(partial(main_kernel, n_tile, n_rep), out_shape=(jax.ShapeD...  157 us
    unnamed x2, local copies, waits for them, and re-layouts  3.85 us

profile of v6, /device:TPU:24, one launch (start us, length us, event | category | flops | bytes accessed | tf_op | source)
XLA Modules:
  0.0 167.7 jit_solution(292326513582682435)
XLA Ops:
  0.7 0.8 compare_bitcast_fusion
  1.5 0.1 fusion.2
  1.6 1.3 copy.15.clips
  2.9 0.8 copy.14
  3.7 0.1 reshape_squeeze.7
  3.8 1.3 add_bitcast_fusion
  5.1 156.7 %conv_norm.1 = (bf16[16,256,256]{2,1,0:T(8,128)(2,1)}, f32[112,256]{1,0:T(8,128)}, f32[8,128]{1,0:T(8,128)}) custom-call(bf16[4,6,8,64,128]{4,3,2,1,0:T(8,128)(2,1)} %bitcast.18, s32[1,128]{1,0:T(1,128)} %get-tuple-element.9.mine, s32[1,128]{1,0:T(1,128)} %get-tuple-element.10.meta, bf16[3456,256]{1,0:T(8,128)(2,1)} %filt_hbm.1, ...), custom_call_target="tpu_custom_call" | custom-call | flops 14495514624 | bytes 16777216 | tf_op jit(solution)/shard_map/conv_norm/pallas_call | solution.py:626
  161.8 0.7 slice.13
  162.5 0.6 reshape.12
  163.1 1.6 constant_dynamic-slice_fusion
  164.6 3.1 %copy.17 = bf16[1,1,16,256,256]{4,3,2,1,0:T(8,128)(2,1)} copy(bf16[1,1,16,256,256]{4,3,2,1,0:T(8,128)(2,1)} %bitcast.15) | data formatting | bytes 4194304
  (4 shorter events, 0.0 us)
